TPU v7x, 32 devices: a whole 2x2x4 slice. The times are simulated.
32 devices in a mesh: mem: 8 (over y, x, core), seq: 4 (over z).
Axes of the slice: x: 2, y: 2, z: 4, core: 2. Of those that a mesh axis runs over, the one named last changes fastest.
Arguments:
- hidden_in: bfloat16 [8, 1024, 768], P('mem', 'seq'), may hold values from -6 to 6
- memory: bfloat16 [4, 768, 768], P(None, 'mem'), may hold values from -6 to 6
- cotangent: bfloat16 [8, 1024, 768], P('mem', 'seq'), may hold values from -6 to 6
- norm_self: bfloat16 [768], P(('mem', 'seq')), may hold values from 0.5 to 1.5
- query_self: bfloat16 [768, 768], P(('mem', 'seq')), may hold values from -0.21875 to 0.21875
- key_self: bfloat16 [768, 768], P(('mem', 'seq')), may hold values from -0.21875 to 0.21875
- value_self: bfloat16 [768, 768], P(('mem', 'seq')), may hold values from -0.21875 to 0.21875
- output_self: bfloat16 [768, 768], P(('mem', 'seq')), may hold values from -0.875 to 0.875
- norm_cross: bfloat16 [768], P(('mem', 'seq')), may hold values from 0.5 to 1.5
- query_cross: bfloat16 [768, 768], P(('mem', 'seq')), may hold values from -0.21875 to 0.21875
- key_cross: bfloat16 [768, 768], P(('mem', 'seq')), may hold values from -0.21875 to 0.21875
- value_cross: bfloat16 [768, 768], P(('mem', 'seq')), may hold values from -0.21875 to 0.21875
- output_cross: bfloat16 [768, 768], P(('mem', 'seq')), may hold values from -0.875 to 0.875
- norm_feed: bfloat16 [768], P(('mem', 'seq')), may hold values from 0.5 to 1.5
- gate_weight: bfloat16 [768, 2048], P(('mem', 'seq')), may hold values from -0.21875 to 0.21875
- up_weight: bfloat16 [768, 2048], P(('mem', 'seq')), may hold values from -0.21875 to 0.21875
- down_weight: bfloat16 [2048, 768], P(('mem', 'seq')), may hold values from -0.125 to 0.125
- block_counts: int32 [8], replicated, may hold values from 1 to 8, 32 in all
- memory_tail: int32 [8], replicated, may hold values from 1 to 96
- row_example: int32 [8], replicated, may hold values from 0 to 7, each once
Outputs:
- layer_out: bfloat16 [8, 1024, 768], P('mem', 'seq')
- hidden_grad: bfloat16 [8, 1024, 768], P('mem', 'seq')
- memory_grad: bfloat16 [4, 768, 768], P('seq', 'mem')
- norm_self_grad: float32 [768], P(('mem', 'seq'))
- query_self_grad: float32 [768, 768], P(('mem', 'seq'))
- key_self_grad: float32 [768, 768], P(('mem', 'seq'))
- value_self_grad: float32 [768, 768], P(('mem', 'seq'))
- output_self_grad: float32 [768, 768], P(('mem', 'seq'))
- norm_cross_grad: float32 [768], P(('mem', 'seq'))
- query_cross_grad: float32 [768, 768], P(('mem', 'seq'))
- key_cross_grad: float32 [768, 768], P(('mem', 'seq'))
- value_cross_grad: float32 [768, 768], P(('mem', 'seq'))
- output_cross_grad: float32 [768, 768], P(('mem', 'seq'))
- norm_feed_grad: float32 [768], P(('mem', 'seq'))
- gate_weight_grad: float32 [768, 2048], P(('mem', 'seq'))
- up_weight_grad: float32 [768, 2048], P(('mem', 'seq'))
- down_weight_grad: float32 [2048, 768], P(('mem', 'seq'))
Inputs may be any that keep to these rules, and one draw needn't show every extreme that they name: block_counts sums to 32; the largest equals 8. `row_example`: each example stands in exactly one row.
All inputs are finite; a program needn't handle non-finite values.
Results may differ from a plain program's by a relative error of at most 0.025.
Values may be sent and summed in bfloat16 or wider, within the bound.
No kernel may reach another device: no remote copies, remote signals or barrier semaphores. Data moves between devices by JAX's collectives and lax.ppermute only.
A program may use at most 256 MiB of HBM per device.

v0:
```python
import jax
import jax.numpy as jnp
from jax import lax
from jax.sharding import PartitionSpec as P

HEADS = 12
HEAD_DIM = 64


def product(left, right):
    return jnp.dot(left, right, preferred_element_type=jnp.float32)


def left_product(left, right):
    return lax.dot_general(
        left, right, (((0,), (0,)), ((), ())), preferred_element_type=jnp.float32
    )


def right_product(left, right):
    return lax.dot_general(
        left, right, (((1,), (1,)), ((), ())), preferred_element_type=jnp.float32
    )


def rms_norm(hidden, gain):
    return hidden * lax.rsqrt(jnp.mean(hidden * hidden, axis=-1, keepdims=True) + 1e-06) * gain


def gelu_tanh(values):
    return (
        0.5
        * values
        * (1.0 + jnp.tanh(0.7978845608028654 * (values + 0.044715 * values * values * values)))
    )


def gated_unit(gate, upper):
    return gelu_tanh(gate) * upper


def norm_backward(hidden, gain, upstream):
    outputs, pullback = jax.vjp(rms_norm, hidden, gain)
    return pullback(upstream)


def block_tables(block_counts, memory_tail, blocks, block_width):
    ends = jnp.cumsum(block_counts)
    examples = jnp.arange(block_counts.shape[0], dtype=jnp.int32)
    block_owner = jnp.sum((ends[None, :] <= blocks[:, None]).astype(jnp.int32), axis=1)
    is_last = jnp.any(ends[None, :] - 1 == blocks[:, None], axis=1)
    tail_size = jnp.sum(
        jnp.where(examples[None, :] == block_owner[:, None], memory_tail[None, :], 0), axis=1
    )
    places = jnp.arange(block_width, dtype=jnp.int32)
    key_live = jnp.logical_or(
        jnp.logical_not(is_last)[:, None], places[None, :] < tail_size[:, None]
    )
    return (jnp.repeat(block_owner, block_width), key_live.reshape(-1))


def local(
    hidden_in,
    memory,
    cotangent,
    norm_self,
    query_self,
    key_self,
    value_self,
    output_self,
    norm_cross,
    query_cross,
    key_cross,
    value_cross,
    output_cross,
    norm_feed,
    gate_weight,
    up_weight,
    down_weight,
    block_counts,
    memory_tail,
    row_example,
):
    (
        gain_self,
        query_full,
        key_full,
        value_full,
        output_full,
        gain_cross,
        cross_query,
        cross_key,
        cross_value,
        cross_output,
        gain_feed,
        gate_full,
        upper_full,
        down_full,
    ) = (
        lax.all_gather(norm_self, ("mem", "seq"), axis=0, tiled=True),
        lax.all_gather(query_self, ("mem", "seq"), axis=0, tiled=True),
        lax.all_gather(key_self, ("mem", "seq"), axis=0, tiled=True),
        lax.all_gather(value_self, ("mem", "seq"), axis=0, tiled=True),
        lax.all_gather(output_self, ("mem", "seq"), axis=0, tiled=True),
        lax.all_gather(norm_cross, ("mem", "seq"), axis=0, tiled=True),
        lax.all_gather(query_cross, ("mem", "seq"), axis=0, tiled=True),
        lax.all_gather(key_cross, ("mem", "seq"), axis=0, tiled=True),
        lax.all_gather(value_cross, ("mem", "seq"), axis=0, tiled=True),
        lax.all_gather(output_cross, ("mem", "seq"), axis=0, tiled=True),
        lax.all_gather(norm_feed, ("mem", "seq"), axis=0, tiled=True),
        lax.all_gather(gate_weight, ("mem", "seq"), axis=0, tiled=True),
        lax.all_gather(up_weight, ("mem", "seq"), axis=0, tiled=True),
        lax.all_gather(down_weight, ("mem", "seq"), axis=0, tiled=True),
    )
    mem_count = lax.axis_size("mem")
    seq_place = lax.axis_index("seq")
    mem_place = lax.axis_index("mem")
    own_rows = hidden_in.shape[1]
    inner_width = HEADS * HEAD_DIM
    scaling = HEAD_DIM ** (-0.5)
    gain_self32 = gain_self.astype(jnp.float32)
    gain_cross32 = gain_cross.astype(jnp.float32)
    gain_feed32 = gain_feed.astype(jnp.float32)
    incoming = hidden_in[0].astype(jnp.float32)
    self_low = rms_norm(incoming, gain_self32).astype(jnp.bfloat16)
    query_low = product(self_low, query_full).astype(jnp.bfloat16)
    key_low = product(self_low, key_full).astype(jnp.bfloat16)
    value_low = product(self_low, value_full).astype(jnp.bfloat16)
    key_cycle, value_cycle = (
        lax.all_gather(key_low, "seq", axis=0, tiled=True),
        lax.all_gather(value_low, "seq", axis=0, tiled=True),
    )
    total_len = key_cycle.shape[0]
    query_three = query_low.reshape(own_rows, HEADS, HEAD_DIM)
    query_places = seq_place * own_rows + jnp.arange(own_rows, dtype=jnp.int32)
    causal = jnp.arange(total_len, dtype=jnp.int32)[None, :] <= query_places[:, None]

    def self_chance(key_rows):
        scores = (
            jnp.einsum(
                "qhd,khd->hqk",
                query_three,
                key_rows.reshape(total_len, HEADS, HEAD_DIM),
                preferred_element_type=jnp.float32,
            )
            * scaling
        )
        return jax.nn.softmax(jnp.where(causal[None], scores, -1e30), axis=-1)

    chance = self_chance(key_cycle)
    chance_low = chance.astype(jnp.bfloat16)
    attended = jnp.einsum(
        "hqk,khd->qhd",
        chance_low,
        value_cycle.reshape(total_len, HEADS, HEAD_DIM),
        preferred_element_type=jnp.float32,
    ).reshape(own_rows, inner_width)
    attended_low = attended.astype(jnp.bfloat16)
    after_self = incoming + right_product(attended_low, output_full)
    cross_low = rms_norm(after_self, gain_cross32).astype(jnp.bfloat16)
    cquery_low = product(cross_low, cross_query).astype(jnp.bfloat16)
    slots = memory.shape[0]
    block_width = memory.shape[1]
    memory_rows = memory.reshape(slots * block_width, memory.shape[2])
    mem_keys = product(memory_rows, cross_key).astype(jnp.bfloat16)
    mem_values = product(memory_rows, cross_value).astype(jnp.bfloat16)
    keys_slot = mem_keys.reshape(slots, block_width, HEADS, HEAD_DIM)
    values_slot = mem_values.reshape(slots, block_width, HEADS, HEAD_DIM)
    local_blocks = jnp.arange(slots, dtype=jnp.int32) * mem_count + mem_place
    key_owner, key_live = block_tables(block_counts, memory_tail, local_blocks, block_width)
    slot_owner = key_owner.reshape(slots, block_width)[:, 0]
    live_slots = key_live.reshape(slots, block_width)
    row_places = jnp.arange(mem_count, dtype=jnp.int32)
    slot_row = jnp.sum(
        jnp.where(row_example[None, :] == slot_owner[:, None], row_places[None, :], 0), axis=1
    )
    row_pick = row_places[None, :] == slot_row[:, None]
    pick_float = row_pick.astype(jnp.float32)

    def to_table(values):
        return jnp.einsum("sg,sqi->gqi", pick_float, values, precision=lax.Precision.HIGHEST)

    queries_all = lax.all_gather(cquery_low, "mem", axis=0, tiled=True)
    all_rows = queries_all.shape[0]
    slot_queries = queries_all.reshape(mem_count, own_rows, HEADS, HEAD_DIM)[slot_row]
    scores = (
        jnp.einsum("sqhd,skhd->shqk", slot_queries, keys_slot, preferred_element_type=jnp.float32)
        * scaling
    )
    scores = jnp.where(live_slots[:, None, None, :], scores, -1e30)
    slot_peak_local = jnp.transpose(jnp.max(scores, axis=3), (0, 2, 1))
    peak_table = jnp.max(
        jnp.where(row_pick[:, :, None, None], slot_peak_local[:, None], -1e30), axis=0
    )
    row_peak = lax.pmax(peak_table.reshape(all_rows, HEADS).astype(jnp.bfloat16), "mem").astype(
        jnp.float32
    )
    slot_peak = row_peak.reshape(mem_count, own_rows, HEADS)[slot_row]
    powers = jnp.where(
        live_slots[:, None, None, :],
        jnp.exp(scores - jnp.transpose(slot_peak, (0, 2, 1))[:, :, :, None]),
        0.0,
    )
    powers_low = powers.astype(jnp.bfloat16)
    slot_totals = jnp.transpose(jnp.sum(powers, axis=3), (0, 2, 1))
    slot_summed = jnp.einsum(
        "shqk,skhd->sqhd", powers_low, values_slot, preferred_element_type=jnp.float32
    ).reshape(slots, own_rows, inner_width)
    summed_own, totals_own = (
        lax.psum_scatter(
            to_table(slot_summed).reshape(all_rows, inner_width),
            "mem",
            scatter_dimension=0,
            tiled=True,
        ),
        lax.psum_scatter(
            to_table(slot_totals).reshape(all_rows, HEADS), "mem", scatter_dimension=0, tiled=True
        ),
    )
    attended_cross = (
        summed_own.reshape(own_rows, HEADS, HEAD_DIM) / totals_own[:, :, None]
    ).reshape(own_rows, inner_width)
    attended_cross_low = attended_cross.astype(jnp.bfloat16)
    after_cross = after_self + right_product(attended_cross_low, cross_output)
    feed_low = rms_norm(after_cross, gain_feed32).astype(jnp.bfloat16)
    gate = product(feed_low, gate_full)
    upper = product(feed_low, upper_full)
    activated_low = gated_unit(gate, upper).astype(jnp.bfloat16)
    layer_out = (after_cross + product(activated_low, down_full)).astype(jnp.bfloat16)
    upstream_out = cotangent[0].astype(jnp.float32)
    upstream_low = cotangent[0]
    down_grad = left_product(activated_low, upstream_low)
    activated_grad = right_product(upstream_low, down_full)
    unit_out, unit_pull = jax.vjp(gated_unit, gate, upper)
    gate_grad, upper_grad = unit_pull(activated_grad)
    gate_grad_low = gate_grad.astype(jnp.bfloat16)
    upper_grad_low = upper_grad.astype(jnp.bfloat16)
    gate_weight_grad = left_product(feed_low, gate_grad_low)
    up_weight_grad = left_product(feed_low, upper_grad_low)
    feed_normed_grad = right_product(gate_grad_low, gate_full) + right_product(
        upper_grad_low, upper_full
    )
    feed_hidden_grad, gain_feed_grad = norm_backward(after_cross, gain_feed32, feed_normed_grad)
    cross_hidden_grad = upstream_out + feed_hidden_grad
    cross_upstream_low = cross_hidden_grad.astype(jnp.bfloat16)
    output_cross_grad = left_product(cross_upstream_low, attended_cross_low)
    cross_attended_grad = product(cross_upstream_low, cross_output).astype(jnp.bfloat16)
    spread_own = jnp.sum(
        cross_attended_grad.astype(jnp.float32).reshape(own_rows, HEADS, HEAD_DIM)
        * attended_cross.reshape(own_rows, HEADS, HEAD_DIM),
        axis=2,
    )
    stats_own = jnp.concatenate([totals_own, spread_own], axis=1)
    grads_all = lax.all_gather(cross_attended_grad, "mem", axis=0, tiled=True)
    stats_all = lax.all_gather(stats_own, "mem", axis=0, tiled=True)
    slot_upstream = grads_all.reshape(mem_count, own_rows, HEADS, HEAD_DIM)[slot_row]
    slot_stats = stats_all.reshape(mem_count, own_rows, 2 * HEADS)[slot_row]
    stat_totals = slot_stats[:, :, :HEADS]
    stat_spread = slot_stats[:, :, HEADS:]
    scaled_up = slot_upstream.astype(jnp.float32) / stat_totals[:, :, :, None]
    scaled_high = scaled_up.astype(jnp.bfloat16)
    scaled_rest = (scaled_up - scaled_high.astype(jnp.float32)).astype(jnp.bfloat16)
    mem_value_sum = jnp.einsum(
        "shqk,sqhd->skhd", powers_low, scaled_high, preferred_element_type=jnp.float32
    ) + jnp.einsum("shqk,sqhd->skhd", powers_low, scaled_rest, preferred_element_type=jnp.float32)
    inner_terms = jnp.einsum(
        "sqhd,skhd->shqk", slot_upstream, values_slot, preferred_element_type=jnp.float32
    )
    score_grad = (
        powers
        * (inner_terms - jnp.transpose(stat_spread, (0, 2, 1))[:, :, :, None])
        / jnp.transpose(stat_totals, (0, 2, 1))[:, :, :, None]
    )
    score_low = (score_grad * scaling).astype(jnp.bfloat16)
    slot_query_grad = jnp.einsum(
        "shqk,skhd->sqhd", score_low, keys_slot, preferred_element_type=jnp.float32
    ).reshape(slots, own_rows, inner_width)
    mem_key_sum = jnp.einsum(
        "shqk,sqhd->skhd", score_low, slot_queries, preferred_element_type=jnp.float32
    )
    cquery_grad = lax.psum_scatter(
        to_table(slot_query_grad).reshape(all_rows, inner_width),
        "mem",
        scatter_dimension=0,
        tiled=True,
    )
    cquery_grad_low = cquery_grad.astype(jnp.bfloat16)
    query_cross_grad = left_product(cross_low, cquery_grad_low)
    cross_normed_grad = right_product(cquery_grad_low, cross_query)
    mem_stacked = jnp.concatenate(
        [mem_key_sum.reshape(-1, inner_width), mem_value_sum.reshape(-1, inner_width)], axis=1
    )
    mem_share = lax.psum_scatter(
        mem_stacked.reshape(slots, block_width, 2 * inner_width).astype(jnp.bfloat16),
        "seq",
        scatter_dimension=0,
        tiled=True,
    ).astype(jnp.float32)
    share_slots = mem_share.shape[0]
    mem_share_low = mem_share.reshape(share_slots * block_width, 2 * inner_width).astype(
        jnp.bfloat16
    )
    mkey_grad_low = mem_share_low[:, :inner_width]
    mvalue_grad_low = mem_share_low[:, inner_width:]
    memory_part = lax.dynamic_slice_in_dim(memory, seq_place * share_slots, share_slots, 0).reshape(
        share_slots * block_width, memory.shape[2]
    )
    key_cross_grad = left_product(memory_part, mkey_grad_low)
    value_cross_grad = left_product(memory_part, mvalue_grad_low)
    memory_grad = (
        (right_product(mkey_grad_low, cross_key) + right_product(mvalue_grad_low, cross_value))
        .astype(jnp.bfloat16)
        .reshape(share_slots, block_width, memory.shape[2])
    )
    cross_norm_hidden, gain_cross_grad = norm_backward(after_self, gain_cross32, cross_normed_grad)
    self_hidden_grad = cross_hidden_grad + cross_norm_hidden
    self_upstream_low = self_hidden_grad.astype(jnp.bfloat16)
    output_self_grad = left_product(self_upstream_low, attended_low)
    self_attended_grad = product(self_upstream_low, output_full).astype(jnp.bfloat16)
    upstream_three = self_attended_grad.reshape(own_rows, HEADS, HEAD_DIM)
    key_back, value_back = (key_cycle, value_cycle)
    chance_back = self_chance(key_back)
    chance_back_low = chance_back.astype(jnp.bfloat16)
    inner_self = jnp.einsum(
        "qhd,khd->hqk",
        upstream_three,
        value_back.reshape(total_len, HEADS, HEAD_DIM),
        preferred_element_type=jnp.float32,
    )
    spread_self = jnp.sum(chance_back * inner_self, axis=2, keepdims=True)
    score_self_low = (chance_back * (inner_self - spread_self) * scaling).astype(jnp.bfloat16)
    query_grad_low = (
        jnp.einsum(
            "hqk,khd->qhd",
            score_self_low,
            key_back.reshape(total_len, HEADS, HEAD_DIM),
            preferred_element_type=jnp.float32,
        )
        .reshape(own_rows, inner_width)
        .astype(jnp.bfloat16)
    )
    key_term = jnp.einsum(
        "hqk,qhd->khd", score_self_low, query_three, preferred_element_type=jnp.float32
    ).reshape(own_rows * lax.axis_size("seq"), inner_width)
    value_term = jnp.einsum(
        "hqk,qhd->khd", chance_back_low, upstream_three, preferred_element_type=jnp.float32
    ).reshape(own_rows * lax.axis_size("seq"), inner_width)
    self_kv_grad = lax.psum_scatter(
        jnp.concatenate([key_term, value_term], axis=1).astype(jnp.bfloat16),
        "seq",
        scatter_dimension=0,
        tiled=True,
    )
    key_grad_low = self_kv_grad[:, :inner_width]
    value_grad_low = self_kv_grad[:, inner_width:]
    query_self_grad = left_product(self_low, query_grad_low)
    key_self_grad = left_product(self_low, key_grad_low)
    value_self_grad = left_product(self_low, value_grad_low)
    self_normed_grad = (
        right_product(query_grad_low, query_full)
        + right_product(key_grad_low, key_full)
        + right_product(value_grad_low, value_full)
    )
    self_norm_hidden, gain_self_grad = norm_backward(incoming, gain_self32, self_normed_grad)
    hidden_grad = (self_hidden_grad + self_norm_hidden).astype(jnp.bfloat16)
    finals = (
        lax.psum_scatter(gain_self_grad, ("mem", "seq"), scatter_dimension=0, tiled=True),
        lax.psum_scatter(query_self_grad, ("mem", "seq"), scatter_dimension=0, tiled=True),
        lax.psum_scatter(key_self_grad, ("mem", "seq"), scatter_dimension=0, tiled=True),
        lax.psum_scatter(value_self_grad, ("mem", "seq"), scatter_dimension=0, tiled=True),
        lax.psum_scatter(output_self_grad, ("mem", "seq"), scatter_dimension=0, tiled=True),
        lax.psum_scatter(gain_cross_grad, ("mem", "seq"), scatter_dimension=0, tiled=True),
        lax.psum_scatter(query_cross_grad, ("mem", "seq"), scatter_dimension=0, tiled=True),
        lax.psum_scatter(key_cross_grad, ("mem", "seq"), scatter_dimension=0, tiled=True),
        lax.psum_scatter(value_cross_grad, ("mem", "seq"), scatter_dimension=0, tiled=True),
        lax.psum_scatter(output_cross_grad, ("mem", "seq"), scatter_dimension=0, tiled=True),
        lax.psum_scatter(gain_feed_grad, ("mem", "seq"), scatter_dimension=0, tiled=True),
        lax.psum_scatter(gate_weight_grad, ("mem", "seq"), scatter_dimension=0, tiled=True),
        lax.psum_scatter(up_weight_grad, ("mem", "seq"), scatter_dimension=0, tiled=True),
        lax.psum_scatter(down_grad, ("mem", "seq"), scatter_dimension=0, tiled=True),
    )
    return (
        layer_out[None],
        hidden_grad[None],
        memory_grad,
        finals[0],
        finals[1],
        finals[2],
        finals[3],
        finals[4],
        finals[5],
        finals[6],
        finals[7],
        finals[8],
        finals[9],
        finals[10],
        finals[11],
        finals[12],
        finals[13],
    )


def solution(mesh):
    in_specs = (
        P("mem", "seq", None),
        P(None, "mem", None),
        P("mem", "seq", None),
        P(("mem", "seq")),
        P(("mem", "seq"), None),
        P(("mem", "seq"), None),
        P(("mem", "seq"), None),
        P(("mem", "seq"), None),
        P(("mem", "seq")),
        P(("mem", "seq"), None),
        P(("mem", "seq"), None),
        P(("mem", "seq"), None),
        P(("mem", "seq"), None),
        P(("mem", "seq")),
        P(("mem", "seq"), None),
        P(("mem", "seq"), None),
        P(("mem", "seq"), None),
        P(),
        P(),
        P(),
    )
    out_specs = (
        P("mem", "seq", None),
        P("mem", "seq", None),
        P("seq", "mem", None),
        P(("mem", "seq")),
        P(("mem", "seq"), None),
        P(("mem", "seq"), None),
        P(("mem", "seq"), None),
        P(("mem", "seq"), None),
        P(("mem", "seq")),
        P(("mem", "seq"), None),
        P(("mem", "seq"), None),
        P(("mem", "seq"), None),
        P(("mem", "seq"), None),
        P(("mem", "seq")),
        P(("mem", "seq"), None),
        P(("mem", "seq"), None),
        P(("mem", "seq"), None),
    )
    return jax.shard_map(local, mesh=mesh, in_specs=in_specs, out_specs=out_specs, check_vma=False)
```

profile of v0, /device:TPU:0, one launch (start us, length us, event | category | flops | bytes accessed | tf_op | source)
XLA Modules:
  0.0 2370.2 jit_solution(7341512516802364178)
XLA Ops:
  12.0 42.1 %all-reduce.7 = (bf16[768]{0:T(1024)(128)(2,1)S(1)}, bf16[768]{0:T(1024)(128)(2,1)S(1)}, bf16[768]{0:T(1024)(128)(2,1)}) all-reduce(bf16[768]{0:T(1024)(128)(2,1)S(1)} %dynamic-update-slice, bf16[768]{0:T(1024)(128)(2,1)S(1)} %dynamic-update-slice.1, bf16[768]{0:T(1024)(128)(2,1)S(1)} %dynamic-update-slice.2), channel_id=1, replica_groups=mesh['mem'=8,'seq'=4] {'mem','seq'}, use_global_device_ids=true, to_apply=%add | all-reduce | flops 2304 | bytes 9216
  70.4 53.1 %all-gather.16.cloned.1.call-done = bf16[768,768]{1,0:T(8,128)(2,1)} async-done(((bf16[24,768]{1,0:T(8,128)(2,1)}), bf16[768,768]{1,0:T(8,128)(2,1)}) %all-gather.16.cloned.1.call-update) | async-done | bytes 1179664 | tf_op jit(solution)/shard_map/all_gather | solution.py:103
  129.9 49.5 %all-gather.20.cloned.1.call-done = bf16[768,768]{1,0:T(8,128)(2,1)} async-done(((bf16[24,768]{1,0:T(8,128)(2,1)}), bf16[768,768]{1,0:T(8,128)(2,1)}) %all-gather.20.cloned.1.call-update) | async-done | bytes 1179664 | tf_op jit(solution)/shard_map/all_gather | solution.py:101
  181.4 36.1 %all-gather.24.cloned.1.call-done = bf16[1024,768]{1,0:T(8,128)(2,1)} async-done(((bf16[256,768]{1,0:T(8,128)(2,1)}), bf16[1024,768]{1,0:T(8,128)(2,1)}) %all-gather.24.cloned.1.call-update) | async-done | bytes 1572880 | tf_op jit(solution)/shard_map/all_gather | solution.py:130
  226.7 28.8 %all-gather.18.cloned.1.call-done = bf16[1024,768]{1,0:T(8,128)(2,1)} async-done(((bf16[256,768]{1,0:T(8,128)(2,1)}), bf16[1024,768]{1,0:T(8,128)(2,1)}) %all-gather.18.cloned.1.call-update) | async-done | bytes 1572880 | tf_op jit(solution)/shard_map/all_gather | solution.py:131
  265.2 45.9 %all-gather.26.cloned.1.call-done = bf16[768,768]{1,0:T(8,128)(2,1)} async-done(((bf16[24,768]{1,0:T(8,128)(2,1)}), bf16[768,768]{1,0:T(8,128)(2,1)}) %all-gather.26.cloned.1.call-update) | async-done | bytes 1179664 | tf_op jit(solution)/shard_map/all_gather | solution.py:104
  313.2 53.8 %all-gather.30.cloned.1.call-done = bf16[768,768]{1,0:T(8,128)(2,1)} async-done(((bf16[24,768]{1,0:T(8,128)(2,1)}), bf16[768,768]{1,0:T(8,128)(2,1)}) %all-gather.30.cloned.1.call-update) | async-done | bytes 1179664 | tf_op jit(solution)/shard_map/all_gather | solution.py:106
  372.3 50.6 %all-gather.34.cloned.1.call-done = bf16[768,768]{1,0:T(8,128)(2,1)} async-done(((bf16[24,768]{1,0:T(8,128)(2,1)}), bf16[768,768]{1,0:T(8,128)(2,1)}) %all-gather.34.cloned.1.call-update) | async-done | bytes 1179664 | tf_op jit(solution)/shard_map/all_gather | solution.py:107
  427.6 51.1 %all-gather.28.cloned.1.call-done = bf16[768,768]{1,0:T(8,128)(2,1)} async-done(((bf16[24,768]{1,0:T(8,128)(2,1)}), bf16[768,768]{1,0:T(8,128)(2,1)}) %all-gather.28.cloned.1.call-update) | async-done | bytes 1179664 | tf_op jit(solution)/shard_map/all_gather | solution.py:108
  483.5 28.9 %all-gather.32.cloned.1.call-done = bf16[2048,768]{1,0:T(8,128)(2,1)} async-done(((bf16[256,768]{1,0:T(8,128)(2,1)}), bf16[2048,768]{1,0:T(8,128)(2,1)}) %all-gather.32.cloned.1.call-update) | async-done | bytes 3145744 | tf_op jit(solution)/shard_map/all_gather | solution.py:183
  529.5 24.0 %pmax.7 = bf16[8,256,12]{1,0,2:T(8,128)(2,1)S(1)} all-reduce(bf16[8,256,12]{1,0,2:T(8,128)(2,1)S(1)} %select_reduce_fusion), channel_id=1, replica_groups=mesh['mem'=8,'seq'=4] {'mem'}, use_global_device_ids=true, to_apply=%region_11.12 | all-reduce | flops 24576 | bytes 98304 | tf_op jit(solution)/shard_map/pmax | solution.py:195
  580.0 19.9 reduce-scatter.19.cloned.1.call-done
  603.9 61.4 %reduce-scatter.17.cloned.1.call-done = f32[256,768]{1,0:T(8,128)} async-done(((f32[2048,768]{1,0:T(8,128)}), f32[256,768]{1,0:T(8,128)}) %reduce-scatter.17.cloned.1.call-update) | async-done | bytes 786448 | tf_op jit(solution)/shard_map/reduce_scatter | solution.py:210
  666.8 55.4 %all-gather.36.cloned.1.call-done = bf16[768,768]{1,0:T(8,128)(2,1)} async-done(((bf16[24,768]{1,0:T(8,128)(2,1)}), bf16[768,768]{1,0:T(8,128)(2,1)}) %all-gather.36.cloned.1.call-update) | async-done | bytes 1179664 | tf_op jit(solution)/shard_map/all_gather | solution.py:109
  725.1 57.9 %all-gather.38.cloned.1.call-done = bf16[768,2048]{1,0:T(8,128)(2,1)} async-done(((bf16[24,2048]{1,0:T(8,128)(2,1)}), bf16[768,2048]{1,0:T(8,128)(2,1)}) %all-gather.38.cloned.1.call-update) | async-done | bytes 3145744 | tf_op jit(solution)/shard_map/all_gather | solution.py:111
  787.2 56.5 %all-gather.40.cloned.1.call-done = bf16[768,2048]{1,0:T(8,128)(2,1)} async-done(((bf16[24,2048]{1,0:T(8,128)(2,1)}), bf16[768,2048]{1,0:T(8,128)(2,1)}) %all-gather.40.cloned.1.call-update) | async-done | bytes 3145744 | tf_op jit(solution)/shard_map/all_gather | solution.py:112
  847.8 56.5 %all-gather.42.cloned.1.call-done = bf16[2048,768]{1,0:T(8,128)(2,1)} async-done(((bf16[64,768]{1,0:T(8,128)(2,1)}), bf16[2048,768]{1,0:T(8,128)(2,1)}) %all-gather.42.cloned.1.call-update) | async-done | bytes 3145744 | tf_op jit(solution)/shard_map/all_gather | solution.py:113
  993.9 55.2 %reduce-scatter.21.cloned.1.call-done = f32[256,768]{1,0:T(8,128)} async-done(((f32[2048,768]{1,0:T(8,128)}), f32[256,768]{1,0:T(8,128)}) %reduce-scatter.21.cloned.1.call-update) | async-done | bytes 786448 | tf_op jit(solution)/shard_map/reduce_scatter | solution.py:281
  1063.5 34.0 %fusion.29 = bf16[12,64,1024]{2,1,0:T(8,128)(2,1)} fusion(bf16[256,12,64]{0,2,1:T(8,128)(2,1)} %bitcast.237, f32[12,256,1024]{2,1,0:T(8,128)} %fusion.134, f32[12,256,1024]{2,1,0:T(8,128)} %get-tuple-element.40, f32[12,256]{1,0:T(8,128)S(1)} %copy-done.59), kind=kOutput, calls=%fused_computation.45 | convolution fusion | flops 425463808 | bytes 27144192 | tf_op jit(solution)/shard_map/hqk,qhd->khd/dot_general | solution.py:342
  1134.1 26.2 %fusion.42 = bf16[12,64,256]{2,1,0:T(8,128)(2,1)S(1)} fusion(bf16[1024,12,64]{0,2,1:T(8,128)(2,1)} %bitcast.225, f32[12,256,1024]{2,1,0:T(8,128)} %fusion.134, f32[12,256,1024]{2,1,0:T(8,128)} %get-tuple-element.40, f32[12,256]{1,0:T(8,128)S(1)} %copy-done.59), kind=kOutput, calls=%fused_computation.62 | convolution fusion | flops 424873984 | bytes 27144192 | tf_op jit(solution)/shard_map/hqk,khd->qhd/dot_general | solution.py:333
  1180.5 40.5 %all-reduce.6 = (f32[768]{0:T(1024)S(1)}, f32[768]{0:T(1024)S(1)}, f32[768]{0:T(1024)S(1)}) all-reduce(f32[768]{0:T(1024)S(1)} %get-tuple-element.21, f32[768]{0:T(1024)S(1)} %get-tuple-element.19, f32[768]{0:T(1024)S(1)} %get-tuple-element.17), channel_id=7, replica_groups=mesh['mem'=8,'seq'=4] {'mem','seq'}, use_global_device_ids=true, to_apply=%region_25.26.clone | all-reduce | flops 2304 | bytes 18432
  1223.7 48.4 %reduce-scatter.41.cloned.1.call-done = f32[24,768]{1,0:T(8,128)} async-done(((f32[768,768]{1,0:T(8,128)}), f32[24,768]{1,0:T(8,128)}) %reduce-scatter.41.cloned.1.call-update) | async-done | bytes 73744 | tf_op jit(solution)/shard_map/reduce_scatter | solution.py:376
  1272.1 119.6 %reduce-scatter.43.cloned.1.call-done = f32[24,2048]{1,0:T(8,128)} async-done(((f32[768,2048]{1,0:T(8,128)}), f32[24,2048]{1,0:T(8,128)}) %reduce-scatter.43.cloned.1.call-update) | async-done | bytes 196624 | tf_op jit(solution)/shard_map/reduce_scatter | solution.py:378
  1391.7 120.9 %reduce-scatter.45.cloned.1.call-done = f32[24,2048]{1,0:T(8,128)} async-done(((f32[768,2048]{1,0:T(8,128)}), f32[24,2048]{1,0:T(8,128)}) %reduce-scatter.45.cloned.1.call-update) | async-done | bytes 196624 | tf_op jit(solution)/shard_map/reduce_scatter | solution.py:379
  1512.6 119.6 %reduce-scatter.47.cloned.1.call-done = f32[64,768]{1,0:T(8,128)} async-done(((f32[2048,768]{1,0:T(8,128)}), f32[64,768]{1,0:T(8,128)}) %reduce-scatter.47.cloned.1.call-update) | async-done | bytes 196624 | tf_op jit(solution)/shard_map/reduce_scatter | solution.py:380
  1632.2 105.0 %reduce-scatter.37.cloned.1.call-done = f32[24,768]{1,0:T(8,128)} async-done(((f32[768,768]{1,0:T(8,128)}), f32[24,768]{1,0:T(8,128)}) %reduce-scatter.37.cloned.1.call-update) | async-done | bytes 73744 | tf_op jit(solution)/shard_map/reduce_scatter | solution.py:374
  1737.2 103.8 %reduce-scatter.39.cloned.1.call-done = f32[24,768]{1,0:T(8,128)} async-done(((f32[768,768]{1,0:T(8,128)}), f32[24,768]{1,0:T(8,128)}) %reduce-scatter.39.cloned.1.call-update) | async-done | bytes 73744 | tf_op jit(solution)/shard_map/reduce_scatter | solution.py:375
  1841.1 104.5 %reduce-scatter.35.cloned.1.call-done = f32[24,768]{1,0:T(8,128)} async-done(((f32[768,768]{1,0:T(8,128)}), f32[24,768]{1,0:T(8,128)}) %reduce-scatter.35.cloned.1.call-update) | async-done | bytes 73744 | tf_op jit(solution)/shard_map/reduce_scatter | solution.py:373
  1945.6 104.0 %reduce-scatter.33.cloned.1.call-done = f32[24,768]{1,0:T(8,128)} async-done(((f32[768,768]{1,0:T(8,128)}), f32[24,768]{1,0:T(8,128)}) %reduce-scatter.33.cloned.1.call-update) | async-done | bytes 73744 | tf_op jit(solution)/shard_map/reduce_scatter | solution.py:371
  2049.5 104.8 %reduce-scatter.27.cloned.1.call-done = f32[24,768]{1,0:T(8,128)} async-done(((f32[768,768]{1,0:T(8,128)}), f32[24,768]{1,0:T(8,128)}) %reduce-scatter.27.cloned.1.call-update) | async-done | bytes 73744 | tf_op jit(solution)/shard_map/reduce_scatter | solution.py:368
  2154.3 103.9 %reduce-scatter.29.cloned.1.call-done = f32[24,768]{1,0:T(8,128)} async-done(((f32[768,768]{1,0:T(8,128)}), f32[24,768]{1,0:T(8,128)}) %reduce-scatter.29.cloned.1.call-update) | async-done | bytes 73744 | tf_op jit(solution)/shard_map/reduce_scatter | solution.py:369
  2258.2 104.7 %reduce-scatter.31.cloned.1.call-done = f32[24,768]{1,0:T(8,128)} async-done(((f32[768,768]{1,0:T(8,128)}), f32[24,768]{1,0:T(8,128)}) %reduce-scatter.31.cloned.1.call-update) | async-done | bytes 73744 | tf_op jit(solution)/shard_map/reduce_scatter | solution.py:370
  (308 shorter events, 287.7 us)
Async XLA Ops:
  7.2 415.7 %copy-start = (bf16[4,96,768]{2,1,0:T(8,128)(2,1)S(1)}, bf16[4,96,768]{2,1,0:T(8,128)(2,1)}, u32[]{:S(2)}) copy-start(bf16[4,96,768]{2,1,0:T(8,128)(2,1)} %param.21) | copy-start | bytes 1769476
  7.2 60.5 %all-gather.22.cloned.1.call-start = ((), (), s32[]{:S(2)}) async-start(), calls=%async_computation.19 | async-start | bytes 1216512 | tf_op jit(solution)/shard_map/all_gather | solution.py:102
  7.9 115.6 %all-gather.16.cloned.1.call-start = ((), (), s32[]{:S(2)}) async-start(), calls=%async_computation.16 | async-start | bytes 1216512 | tf_op jit(solution)/shard_map/all_gather | solution.py:103
  8.7 170.7 %all-gather.20.cloned.1.call-start = ((), (), s32[]{:S(2)}) async-start(), calls=%async_computation.18 | async-start | bytes 1216512 | tf_op jit(solution)/shard_map/all_gather | solution.py:101
  9.4 208.1 %all-gather.24.cloned.1.call-start = ((), (), s32[]{:S(2)}) async-start(), calls=%async_computation.20 | async-start | bytes 1966080 | tf_op jit(solution)/shard_map/all_gather | solution.py:130
  70.4 185.1 %all-gather.18.cloned.1.call-start = ((), (), s32[]{:S(2)}) async-start(), calls=%async_computation.17 | async-start | bytes 1966080 | tf_op jit(solution)/shard_map/all_gather | solution.py:131
  126.1 185.0 %all-gather.26.cloned.1.call-start = ((), (), s32[]{:S(2)}) async-start(), calls=%async_computation.21 | async-start | bytes 1216512 | tf_op jit(solution)/shard_map/all_gather | solution.py:104
  126.7 240.3 %all-gather.30.cloned.1.call-start = ((), (), s32[]{:S(2)}) async-start(), calls=%async_computation.23 | async-start | bytes 1216512 | tf_op jit(solution)/shard_map/all_gather | solution.py:106
  127.5 295.4 %all-gather.34.cloned.1.call-start = ((), (), s32[]{:S(2)}) async-start(), calls=%async_computation.25 | async-start | bytes 1216512 | tf_op jit(solution)/shard_map/all_gather | solution.py:107
  128.2 350.5 %all-gather.28.cloned.1.call-start = ((), (), s32[]{:S(2)}) async-start(), calls=%async_computation.22 | async-start | bytes 1216512 | tf_op jit(solution)/shard_map/all_gather | solution.py:108
  128.9 383.4 %all-gather.32.cloned.1.call-start = ((), (), s32[]{:S(2)}) async-start(), calls=%async_computation.24 | async-start | bytes 3538944 | tf_op jit(solution)/shard_map/all_gather | solution.py:183
  369.6 230.4 %reduce-scatter.19.cloned.1.call-start = ((), (), s32[]{:S(2)}) async-start(), calls=%async_computation.27 | async-start | bytes 147456 | tf_op jit(solution)/shard_map/reduce_scatter | solution.py:216
  566.4 98.9 %reduce-scatter.17.cloned.1.call-start = ((), (), s32[]{:S(2)}) async-start(), calls=%async_computation.26 | async-start | bytes 7077888 | tf_op jit(solution)/shard_map/reduce_scatter | solution.py:210
  577.0 145.3 %all-gather.36.cloned.1.call-start = ((), (), s32[]{:S(2)}) async-start(), calls=%async_computation.28 | async-start | bytes 1216512 | tf_op jit(solution)/shard_map/all_gather | solution.py:109
  577.7 205.3 %all-gather.38.cloned.1.call-start = ((), (), s32[]{:S(2)}) async-start(), calls=%async_computation.29 | async-start | bytes 3244032 | tf_op jit(solution)/shard_map/all_gather | solution.py:111
  578.3 265.3 %all-gather.40.cloned.1.call-start = ((), (), s32[]{:S(2)}) async-start(), calls=%async_computation.30 | async-start | bytes 3244032 | tf_op jit(solution)/shard_map/all_gather | solution.py:112
  578.9 325.4 %all-gather.42.cloned.1.call-start = ((), (), s32[]{:S(2)}) async-start(), calls=%async_computation.31 | async-start | bytes 3244032 | tf_op jit(solution)/shard_map/all_gather | solution.py:113
  579.5 370.5 %all-gather.44.cloned.1.call-start = ((), (), s32[]{:S(2)}) async-start(), calls=%async_computation.32 | async-start | bytes 3538944 | tf_op jit(solution)/shard_map/all_gather | solution.py:254
  918.1 131.0 %reduce-scatter.21.cloned.1.call-start = ((), (), s32[]{:S(2)}) async-start(), calls=%async_computation.33 | async-start | bytes 7077888 | tf_op jit(solution)/shard_map/reduce_scatter | solution.py:281
  987.2 137.7 %reduce-scatter.25.cloned.1.call-start = ((), (), s32[]{:S(2)}) async-start(), calls=%async_computation.35 | async-start | bytes 1966080 | tf_op jit(solution)/shard_map/reduce_scatter | solution.py:293
  993.8 172.5 %reduce-scatter.23.cloned.1.call-start = ((), (), s32[]{:S(2)}) async-start(), calls=%async_computation.34 | async-start | bytes 3932160 | tf_op jit(solution)/shard_map/reduce_scatter | solution.py:348
  1105.9 166.1 %reduce-scatter.41.cloned.1.call-start = ((), (), s32[]{:S(2)}) async-start(), calls=%async_computation.43 | async-start | bytes 2433024 | tf_op jit(solution)/shard_map/reduce_scatter | solution.py:376
  1108.9 282.8 %reduce-scatter.43.cloned.1.call-start = ((), (), s32[]{:S(2)}) async-start(), calls=%async_computation.44 | async-start | bytes 6488064 | tf_op jit(solution)/shard_map/reduce_scatter | solution.py:378
  1113.9 398.7 %reduce-scatter.45.cloned.1.call-start = ((), (), s32[]{:S(2)}) async-start(), calls=%async_computation.45 | async-start | bytes 6488064 | tf_op jit(solution)/shard_map/reduce_scatter | solution.py:379
  1119.0 513.3 %reduce-scatter.47.cloned.1.call-start = ((), (), s32[]{:S(2)}) async-start(), calls=%async_computation.46 | async-start | bytes 6488064 | tf_op jit(solution)/shard_map/reduce_scatter | solution.py:380
  1124.8 612.4 %reduce-scatter.37.cloned.1.call-start = ((), (), s32[]{:S(2)}) async-start(), calls=%async_computation.41 | async-start | bytes 2433024 | tf_op jit(solution)/shard_map/reduce_scatter | solution.py:374
  1127.9 713.2 %reduce-scatter.39.cloned.1.call-start = ((), (), s32[]{:S(2)}) async-start(), calls=%async_computation.42 | async-start | bytes 2433024 | tf_op jit(solution)/shard_map/reduce_scatter | solution.py:375
  1129.9 815.7 %reduce-scatter.35.cloned.1.call-start = ((), (), s32[]{:S(2)}) async-start(), calls=%async_computation.40 | async-start | bytes 2433024 | tf_op jit(solution)/shard_map/reduce_scatter | solution.py:373
  1132.0 917.6 %reduce-scatter.33.cloned.1.call-start = ((), (), s32[]{:S(2)}) async-start(), calls=%async_computation.39 | async-start | bytes 2433024 | tf_op jit(solution)/shard_map/reduce_scatter | solution.py:371
  1134.0 1020.3 %reduce-scatter.27.cloned.1.call-start = ((), (), s32[]{:S(2)}) async-start(), calls=%async_computation.36 | async-start | bytes 2433024 | tf_op jit(solution)/shard_map/reduce_scatter | solution.py:368
  1162.4 1095.8 %reduce-scatter.29.cloned.1.call-start = ((), (), s32[]{:S(2)}) async-start(), calls=%async_computation.37 | async-start | bytes 2433024 | tf_op jit(solution)/shard_map/reduce_scatter | solution.py:369
  1169.4 1193.5 %reduce-scatter.31.cloned.1.call-start = ((), (), s32[]{:S(2)}) async-start(), calls=%async_computation.38 | async-start | bytes 2433024 | tf_op jit(solution)/shard_map/reduce_scatter | solution.py:370
  (59 other events, 1292.6 us)
Sparse Core Ops, SparseCore 0:
  10.8 56.7 all-gather.21
  70.5 53.0 all-gather.15
  126.4 53.0 all-gather.19
  181.4 36.0 all-gather.23
  219.5 35.9 all-gather.17
  258.1 52.9 all-gather.25
  313.9 53.0 all-gather.29
  369.8 53.0 all-gather.33
  425.7 53.0 all-gather.27
  481.0 31.2 all-gather.31
  566.5 33.3 reduce-scatter.18
  603.5 61.7 reduce-scatter.16
  668.1 54.0 all-gather.35
  725.0 57.9 all-gather.37
  785.7 57.8 all-gather.39
  846.4 57.8 all-gather.41
  918.2 31.7 all-gather.43
  987.3 61.7 reduce-scatter.20
  1051.5 35.3 reduce-scatter.24
  1106.1 60.2 reduce-scatter.22
  1173.1 98.9 reduce-scatter.40
  1278.3 113.3 reduce-scatter.42
  1398.8 113.7 reduce-scatter.44
  1518.7 113.5 reduce-scatter.46
  1638.9 98.2 reduce-scatter.36
  1742.9 98.0 reduce-scatter.38
  1847.6 97.9 reduce-scatter.34
  1951.4 98.0 reduce-scatter.32
  2056.3 98.0 reduce-scatter.26
  2160.0 98.1 reduce-scatter.28
  2264.9 97.9 reduce-scatter.30
where the time goes:
time: 2380 us; the launch traced here: 2370 us
  waiting for transfers between devices  1940 us (82%)
  matrix products  202 us (8%)
  blocking collectives  116 us (5%)
  local copies, waits for them, and re-layouts  80.2 us (3%)
    reduce_scatter x1, waiting for transfers between devices, local(): lax.psum_scatter(up_weight_grad, ('mem', 'seq'), scatter_dimension=0, til...  121 us
    reduce_scatter x1, waiting for transfers between devices, local(): lax.psum_scatter(down_grad, ('mem', 'seq'), scatter_dimension=0, tiled=True)  120 us
    reduce_scatter x1, waiting for transfers between devices, local(): lax.psum_scatter(gate_weight_grad, ('mem', 'seq'), scatter_dimension=0, t...  120 us
    reduce_scatter x1, waiting for transfers between devices, local(): lax.psum_scatter(key_cross_grad, ('mem', 'seq'), scatter_dimension=0, til...  105 us
    reduce_scatter x1, waiting for transfers between devices, local(): lax.psum_scatter(query_self_grad, ('mem', 'seq'), scatter_dimension=0, ti...  105 us
    reduce_scatter x1, waiting for transfers between devices, local(): lax.psum_scatter(value_self_grad, ('mem', 'seq'), scatter_dimension=0, ti...  105 us
    reduce_scatter x1, waiting for transfers between devices, local(): lax.psum_scatter(query_cross_grad, ('mem', 'seq'), scatter_dimension=0, t...  105 us
    reduce_scatter x1, waiting for transfers between devices, local(): lax.psum_scatter(output_self_grad, ('mem', 'seq'), scatter_dimension=0, t...  104 us
  transfers between devices with their start and end apart: 31, of which 30 were waited for; matrix products, arithmetic and copies ran while one was open for 9% of the time, Pallas kernels for 0%

commit v1 on v0

v1 whole, which is shorter than its diff:
```python
import functools

import jax
import jax.numpy as jnp
from jax import lax
from jax.experimental import pallas as pl
from jax.experimental.pallas import tpu as pltpu
from jax.sharding import PartitionSpec as P

HEADS = 12
HEAD_DIM = 64
SCALING = HEAD_DIM ** (-0.5)
LANES = 128
MASKED = -1e30
F32 = jnp.float32
BF16 = jnp.bfloat16


def product(left, right):
    return jnp.dot(left, right, preferred_element_type=F32)


def left_product(left, right):
    return lax.dot_general(left, right, (((0,), (0,)), ((), ())), preferred_element_type=F32)


def right_product(left, right):
    return lax.dot_general(left, right, (((1,), (1,)), ((), ())), preferred_element_type=F32)


def gelu_tanh(values):
    return (
        0.5
        * values
        * (1.0 + jnp.tanh(0.7978845608028654 * (values + 0.044715 * values * values * values)))
    )


def gated_unit(gate, upper):
    return gelu_tanh(gate) * upper


def norm_scale(hidden):
    return lax.rsqrt(jnp.mean(hidden * hidden, axis=-1, keepdims=True) + 1e-06)


def norm_hidden_grad(hidden, scale, gain, upstream):
    lifted = upstream * gain
    return scale * lifted - hidden * (scale * scale * scale) * jnp.mean(
        lifted * hidden, axis=-1, keepdims=True
    )


def shift(values, axis, step):
    size = lax.axis_size(axis)
    return lax.ppermute(values, axis, [(i, (i + step) % size) for i in range(size)])


def swap(values, axis, mask):
    size = lax.axis_size(axis)
    return lax.ppermute(values, axis, [(i, i ^ mask) for i in range(size)])


def place_kernel(moves, splits, places, *refs):
    sources = refs[: len(moves)]
    targets = refs[len(moves) : len(moves) + len(splits)]
    done = refs[-1]
    copies = []
    number = 0
    for source, count in zip(sources, moves):
        for block in range(count):
            for target, (first, last) in zip(targets, splits):
                part = source.at[block]
                if len(splits) > 1:
                    part = source.at[block, :, first:last]
                copies.append(
                    pltpu.make_async_copy(part, target.at[places[number]], done.at[len(copies)])
                )
            number += 1
    for copy in copies:
        copy.start()
    for copy in copies:
        copy.wait()


def place(pieces, places, widths=None):
    counts = [piece.shape[0] for piece in pieces]
    total = sum(counts)
    _, height, width = pieces[0].shape
    widths = widths or [width]
    edges = [sum(widths[:i]) for i in range(len(widths) + 1)]
    splits = list(zip(edges[:-1], edges[1:]))
    outs = [jax.ShapeDtypeStruct((total, height, w), pieces[0].dtype) for w in widths]
    size = total * height * width * 2
    result = pl.pallas_call(
        functools.partial(place_kernel, counts, splits),
        out_shape=outs,
        grid_spec=pltpu.PrefetchScalarGridSpec(
            num_scalar_prefetch=1,
            grid=(1,),
            in_specs=[pl.BlockSpec(memory_space=pl.ANY)] * len(pieces),
            out_specs=[
                pl.BlockSpec((total, height, w), lambda i, places: (0, 0, 0)) for w in widths
            ],
            scratch_shapes=[pltpu.SemaphoreType.DMA((total * len(splits),))],
        ),
        compiler_params=pltpu.CompilerParams(vmem_limit_bytes=3 * size + (4 << 20)),
        cost_estimate=pl.CostEstimate(flops=0, bytes_accessed=2 * size, transcendentals=0),
        name="place",
    )(places.astype(jnp.int32), *pieces)
    return result[0] if len(widths) == 1 else result


def after(values, *tokens):
    return lax.optimization_barrier((values,) + tokens)[0]


def gather_seq(values):
    size = lax.axis_size("seq")
    index = lax.axis_index("seq")
    pieces = [values[None]] + [shift(values, "seq", k)[None] for k in range(1, size)]
    return place(pieces, (index - jnp.arange(size)) % size)


def spread_seq(blocks):
    size = lax.axis_size("seq")
    index = lax.axis_index("seq")
    kept = lax.dynamic_index_in_dim(blocks, index, 0, keepdims=False)
    return [kept] + [
        shift(
            lax.dynamic_index_in_dim(blocks, (index + k) % size, 0, keepdims=False), "seq", k
        )
        for k in range(1, size)
    ]


def slot_masks(order):
    count = len(order)
    return [
        sum((((t >> (count - 1 - i)) & 1) << bit) for i, bit in enumerate(order))
        for t in range(1 << count)
    ]


def gather_mem(values, order):
    index = lax.axis_index("mem")
    held = values[None]
    masks = [0]
    for bit in order[:-1]:
        held = jnp.concatenate([held, swap(held, "mem", 1 << bit)], axis=0)
        masks = masks + [mask | (1 << bit) for mask in masks]
    other = swap(held, "mem", 1 << order[-1])
    masks = masks + [mask | (1 << order[-1]) for mask in masks]
    return place([held, other], index ^ jnp.array(masks, jnp.int32))


def scatter_mem(blocks, order):
    held = blocks
    for bit in order:
        half = held.shape[0] // 2
        arrived = swap(held[half:], "mem", 1 << bit)
        held = (held[:half].astype(F32) + arrived.astype(F32)).astype(BF16)
    return held


def scatter_all(blocks, order):
    held = scatter_mem(blocks, order)
    size = lax.axis_size("seq")
    pieces = spread_seq(held.reshape(size, held.shape[0] // size, held.shape[1]))
    return functools.reduce(jnp.add, [piece.astype(F32) for piece in pieces])


def head_mask(shape, head):
    return lax.broadcasted_iota(jnp.int32, shape, 1) // HEAD_DIM == head


def pick_head(values, head):
    return jnp.where(head_mask(values.shape, head), values, jnp.zeros_like(values))


def transposed(values):
    return values.astype(F32).T.astype(values.dtype)


def soft_parts(scores):
    peak = jnp.max(scores, axis=0, keepdims=True)
    powers = jnp.exp(scores - peak)
    return powers, 1.0 / jnp.sum(powers, axis=0, keepdims=True)


def causal_scores(keys, queries, first):
    scores = right_product(keys, queries) * SCALING
    key_place = lax.broadcasted_iota(jnp.int32, scores.shape, 0)
    query_place = lax.broadcasted_iota(jnp.int32, scores.shape, 1) + first
    return jnp.where(key_place <= query_place, scores, MASKED)


def self_forward_kernel(heads, chunk, q_ref, k_ref, v_ref, out_ref):
    values_t = transposed(v_ref[...])
    width = heads * HEAD_DIM
    for first in range(0, q_ref.shape[0], chunk):
        last = first + chunk
        queries = q_ref[first:last]
        parts = []
        for head in range(heads):
            scores = causal_scores(k_ref[:last], pick_head(queries, head), first)
            powers, inverse = soft_parts(scores)
            rows = values_t[head * HEAD_DIM : (head + 1) * HEAD_DIM, :last]
            parts.append(product(rows, powers.astype(BF16)) * inverse)
        out_ref[first:last] = jnp.concatenate(parts, axis=0).T[:, :width].astype(BF16)


def self_backward_kernel(heads, chunk, q_ref, k_ref, v_ref, up_ref, dq_ref, dk_ref, dv_ref, dk_sum, dv_sum):
    keys_t = transposed(k_ref[...])
    dk_sum[...] = jnp.zeros_like(dk_sum)
    dv_sum[...] = jnp.zeros_like(dv_sum)
    width = keys_t.shape[0]
    for first in range(0, q_ref.shape[0], chunk):
        last = first + chunk
        queries = q_ref[first:last]
        upstream = up_ref[first:last]
        parts = []
        for head in range(heads):
            own = pick_head(queries, head)
            up_own = pick_head(upstream, head)
            powers, inverse = soft_parts(causal_scores(k_ref[:last], own, first))
            chance = powers * inverse
            inner = right_product(v_ref[:last], up_own)
            spread = jnp.sum(chance * inner, axis=0, keepdims=True)
            grad = (chance * (inner - spread) * SCALING).astype(BF16)
            dv_sum[:last] += product(chance.astype(BF16), up_own)
            dk_sum[:last] += product(grad, own)
            rows = keys_t[head * HEAD_DIM : (head + 1) * HEAD_DIM, :last]
            parts.append(product(rows, grad))
        rest = jnp.zeros((width - heads * HEAD_DIM, chunk), F32)
        dq_ref[first:last] = jnp.concatenate(parts + [rest], axis=0).T.astype(BF16)
    dk_ref[...] = dk_sum[...].astype(BF16)
    dv_ref[...] = dv_sum[...].astype(BF16)


def cross_scores(keys, queries, live):
    return jnp.where(live > 0, right_product(keys, queries) * SCALING, MASKED)


def cross_forward_kernel(live_ref, q_ref, k_ref, v_ref, out_ref):
    values_t = transposed(v_ref[...])
    queries = q_ref[...]
    live = live_ref[...]
    parts = []
    for head in range(LANES // HEAD_DIM):
        powers, inverse = soft_parts(cross_scores(k_ref[...], pick_head(queries, head), live))
        rows = values_t[head * HEAD_DIM : (head + 1) * HEAD_DIM]
        parts.append(product(rows, powers.astype(BF16)) * inverse)
    out_ref[...] = jnp.concatenate(parts, axis=0).T.astype(BF16)


def cross_backward_kernel(live_ref, q_ref, k_ref, v_ref, up_ref, dq_ref, dk_ref, dv_ref):
    keys_t = transposed(k_ref[...])
    queries = q_ref[...]
    upstream = up_ref[...]
    live = live_ref[...]
    parts, dk, dv = [], 0.0, 0.0
    for head in range(LANES // HEAD_DIM):
        own = pick_head(queries, head)
        up_own = pick_head(upstream, head)
        powers, inverse = soft_parts(cross_scores(k_ref[...], own, live))
        chance = powers * inverse
        inner = right_product(v_ref[...], up_own)
        spread = jnp.sum(chance * inner, axis=0, keepdims=True)
        grad = (chance * (inner - spread) * SCALING).astype(BF16)
        dv = dv + product(chance.astype(BF16), up_own)
        dk = dk + product(grad, own)
        rows = keys_t[head * HEAD_DIM : (head + 1) * HEAD_DIM]
        parts.append(product(rows, grad))
    dq_ref[...] = jnp.concatenate(parts, axis=0).T.astype(BF16)
    dk_ref[...] = dk.astype(BF16)
    dv_ref[...] = dv.astype(BF16)


def vmem(mebibytes):
    return pltpu.CompilerParams(vmem_limit_bytes=mebibytes << 20)


def self_forward(qkv, heads, chunk):
    length, width = qkv.shape[0], qkv.shape[1] // 3
    spec = lambda j: pl.BlockSpec((length, width), lambda i, j=j: (0, j))
    return pl.pallas_call(
        functools.partial(self_forward_kernel, heads, chunk),
        out_shape=jax.ShapeDtypeStruct((length, heads * HEAD_DIM), BF16),
        grid=(1,),
        in_specs=[spec(0), spec(1), spec(2)],
        out_specs=pl.BlockSpec((length, heads * HEAD_DIM), lambda i: (0, 0)),
        compiler_params=vmem(32),
        name="self_forward",
    )(qkv, qkv, qkv)


def self_backward(qkv, upstream, heads, chunk):
    length, width = qkv.shape[0], qkv.shape[1] // 3
    spec = lambda j: pl.BlockSpec((length, width), lambda i, j=j: (0, j))
    whole = jax.ShapeDtypeStruct((length, width), BF16)
    return pl.pallas_call(
        functools.partial(self_backward_kernel, heads, chunk),
        out_shape=(whole, whole, whole),
        grid=(1,),
        in_specs=[spec(0), spec(1), spec(2), spec(0)],
        out_specs=(spec(0), spec(0), spec(0)),
        scratch_shapes=[pltpu.VMEM((length, width), F32), pltpu.VMEM((length, width), F32)],
        compiler_params=vmem(40),
        name="self_backward",
    )(qkv, qkv, qkv, upstream)


def cross_specs(rows, keys):
    return (
        pl.BlockSpec((keys, 1), lambda i: (0, 0)),
        pl.BlockSpec((rows, LANES), lambda i: (0, i)),
        pl.BlockSpec((keys, LANES), lambda i: (0, i)),
    )


def cross_room(keys):
    return vmem(max(24, keys * 8 // 1024 + 8))


def cross_forward(live, queries, keys, values):
    live_spec, row_spec, key_spec = cross_specs(queries.shape[0], keys.shape[0])
    return pl.pallas_call(
        cross_forward_kernel,
        out_shape=jax.ShapeDtypeStruct(queries.shape, BF16),
        grid=(queries.shape[1] // LANES,),
        in_specs=[live_spec, row_spec, key_spec, key_spec],
        out_specs=row_spec,
        compiler_params=cross_room(keys.shape[0]),
        name="cross_forward",
    )(live, queries, keys, values)


def cross_backward(live, queries, keys, values, upstream):
    live_spec, row_spec, key_spec = cross_specs(queries.shape[0], keys.shape[0])
    return pl.pallas_call(
        cross_backward_kernel,
        out_shape=(
            jax.ShapeDtypeStruct(queries.shape, BF16),
            jax.ShapeDtypeStruct(keys.shape, BF16),
            jax.ShapeDtypeStruct(keys.shape, BF16),
        ),
        grid=(queries.shape[1] // LANES,),
        in_specs=[live_spec, row_spec, key_spec, key_spec, row_spec],
        out_specs=(row_spec, key_spec, key_spec),
        compiler_params=cross_room(keys.shape[0]),
        name="cross_backward",
    )(live, queries, keys, values, upstream)


def local(
    hidden_in,
    memory,
    cotangent,
    norm_self,
    query_self,
    key_self,
    value_self,
    output_self,
    norm_cross,
    query_cross,
    key_cross,
    value_cross,
    output_cross,
    norm_feed,
    gate_weight,
    up_weight,
    down_weight,
    block_counts,
    memory_tail,
    row_example,
):
    mem_count, seq_count = lax.axis_size("mem"), lax.axis_size("seq")
    mem_place, seq_place = lax.axis_index("mem"), lax.axis_index("seq")
    rows, width = hidden_in.shape[1], hidden_in.shape[2]
    inner = HEADS * HEAD_DIM
    length = rows * seq_count
    near = HEADS // seq_count
    slim = near * HEAD_DIM
    broad = -(-(slim + 3) // LANES) * LANES
    share = norm_self.shape[0]
    feed_share = down_weight.shape[0]
    hidden_width = gate_weight.shape[1]
    bits = mem_count.bit_length() - 1
    orders = (
        [*range(1, bits), 0],
        [*range(bits - 1, 0, -1), 0],
    )
    back_orders = (
        [0, *range(1, bits)],
        [0, *range(bits - 1, 0, -1)],
    )

    with jax.named_scope("gather_hidden"):
        x_all = gather_seq(hidden_in[0]).reshape(length, width)

    with jax.named_scope("gather_self"):
        gains = jnp.stack([norm_self, norm_cross, norm_feed], axis=1)

        def by_seq(weight):
            return jnp.transpose(weight.reshape(share, seq_count, slim), (1, 0, 2))

        def padded(block, extra):
            return jnp.concatenate([block, extra], axis=2)

        gain_pad = jnp.broadcast_to(
            jnp.concatenate([gains, jnp.zeros((share, broad - slim - 3), BF16)], axis=1)[None],
            (seq_count, share, broad - slim),
        )
        zero_pad = jnp.zeros((seq_count, share, broad - slim), BF16)
        triple = jnp.concatenate(
            [
                padded(by_seq(query_self), gain_pad),
                padded(by_seq(key_self), zero_pad),
                padded(by_seq(value_self), zero_pad),
            ],
            axis=2,
        )
        triple_mine = place(
            [piece[None] for piece in spread_seq(triple)],
            (seq_place - jnp.arange(seq_count)) % seq_count,
        )
        w_self = gather_mem(triple_mine.reshape(seq_count * share, 3 * broad), orders[0])
        w_self = w_self.reshape(width, 3 * broad)
        gains_all = w_self[:, slim : slim + 3].astype(F32).T
        gain_self32, gain_cross32, gain_feed32 = gains_all[0:1], gains_all[1:2], gains_all[2:3]

    def gather_all(shard, order):
        across = gather_seq(shard)
        full = gather_mem(across.reshape(-1, shard.shape[1]), order)
        return full.reshape(-1, shard.shape[1])

    with jax.named_scope("gather_outer"):
        w_outer = gather_all(jnp.concatenate([output_self, query_cross], axis=1), orders[1])
        w_output_self, w_query_cross = w_outer[:, :inner], w_outer[:, inner:]

    with jax.named_scope("gather_memory"):
        ends = jnp.cumsum(block_counts)
        starts = ends - block_counts
        places = jnp.arange(mem_count, dtype=jnp.int32)

        def block_of(example, holder):
            first = starts[example]
            block = first + (holder - first) % mem_count
            return block, block < ends[example]

        pieces = []
        for mask in range(mem_count):
            block, _ = block_of(row_example[mem_place ^ mask], mem_place)
            slot = jnp.clip(block // mem_count, 0, memory.shape[0] - 1)
            piece = lax.dynamic_index_in_dim(memory, slot, 0, keepdims=False)
            pieces.append(swap(piece, "mem", mask) if mask else piece)
        block_width = memory.shape[1]
        keys_in = jnp.concatenate(pieces, axis=0)
        mine = row_example[mem_place]
        owned_block, owned = block_of(mine, mem_place ^ places)
        is_last = owned_block == ends[mine] - 1
        token = jnp.arange(block_width, dtype=jnp.int32)
        live = jnp.logical_and(
            owned[:, None],
            jnp.logical_or(jnp.logical_not(is_last)[:, None], token[None, :] < memory_tail[mine]),
        )
        live = live.astype(F32).reshape(-1, 1)

    with jax.named_scope("gather_cross"):
        w_cross = gather_all(
            jnp.concatenate([key_cross, value_cross, output_cross], axis=1), orders[0]
        )
        w_key_value, w_output_cross = w_cross[:, : 2 * inner], w_cross[:, 2 * inner :]

    with jax.named_scope("gather_feed"):
        w_feed = gather_all(jnp.concatenate([gate_weight, up_weight], axis=1), orders[1])
        w_down = gather_all(down_weight, orders[0])

    with jax.named_scope("self_attention"):
        x32 = x_all.astype(F32)
        scale_all = norm_scale(x32)
        n1_all = (x32 * scale_all * gain_self32).astype(BF16)
        qkv = product(n1_all, w_self).astype(BF16)
        o1 = self_forward(qkv, near, rows)

    def heads_to_rows(values):
        pieces = spread_seq(values.reshape(seq_count, rows, slim))
        stacked = jnp.stack(pieces)
        return jnp.concatenate(
            [
                lax.dynamic_index_in_dim(stacked, (seq_place - j) % seq_count, 0, keepdims=False)
                for j in range(seq_count)
            ],
            axis=1,
        )

    def rows_to_heads(values):
        blocks = jnp.transpose(values.reshape(rows, seq_count, slim), (1, 0, 2))
        return place(
            [piece[None] for piece in spread_seq(blocks)],
            (seq_place - jnp.arange(seq_count)) % seq_count,
        ).reshape(length, slim)

    with jax.named_scope("self_output"):
        a1 = heads_to_rows(o1)
        x_own = hidden_in[0].astype(F32)
        h1 = x_own + right_product(a1, w_output_self)
        scale_cross = norm_scale(h1)
        n2 = (h1 * scale_cross * gain_cross32).astype(BF16)
        q2 = product(n2, w_query_cross).astype(BF16)

    with jax.named_scope("cross_attention"):
        kv2 = product(keys_in, w_key_value).astype(BF16)
        k2, v2 = kv2[:, :inner], kv2[:, inner:]
        a2 = cross_forward(live, q2, k2, v2)
        h2 = h1 + right_product(a2, w_output_cross)

    with jax.named_scope("feed"):
        scale_feed = norm_scale(h2)
        n3 = (h2 * scale_feed * gain_feed32).astype(BF16)
        both = product(n3, w_feed)
        gate, upper = both[:, :hidden_width], both[:, hidden_width:]
        act = gated_unit(gate, upper).astype(BF16)
        layer_out = (h2 + product(act, w_down)).astype(BF16)

    def relative(order):
        masks = jnp.array(slot_masks(order), jnp.int32)
        column = jnp.arange(width, dtype=jnp.int32)
        block = width // mem_count
        source = block * (mem_place ^ jnp.repeat(masks, block)) + column % block
        return (column[:, None] == source[None, :]).astype(BF16)

    pick = [relative(order) for order in back_orders]

    def turned(values, which):
        return product(values, pick[which]).astype(BF16)

    def gain_column(values):
        ones = jnp.ones((values.shape[0], LANES), BF16)
        return left_product(values.astype(BF16), ones)

    with jax.named_scope("feed_back"):
        c3 = cotangent[0]
        act_places = jnp.argsort(mem_place ^ jnp.array(slot_masks(back_orders[0]), jnp.int32))
        g_down = left_product(act, c3).astype(BF16)
        g_down = place([g_down.reshape(mem_count, -1, width)], act_places)
        down_weight_grad = scatter_all(g_down.reshape(-1, width), back_orders[0])
        dact = right_product(c3, w_down)
        _, unit_pull = jax.vjp(gated_unit, gate, upper)
        dgate, dupper = unit_pull(dact)
        dboth = jnp.concatenate([dgate.astype(BF16), dupper.astype(BF16)], axis=1)
        n3_rel = turned(n3, 1)
        g_feed = scatter_all(left_product(n3_rel, dboth).astype(BF16), back_orders[1])
        dn3 = right_product(dboth, w_feed)
        dh2 = c3.astype(F32) + norm_hidden_grad(h2, scale_feed, gain_feed32, dn3)
        gain_feed_terms = jnp.sum(dn3 * h2 * scale_feed, axis=0)

    with jax.named_scope("cross_back"):
        c2 = dh2.astype(BF16)
        da2 = product(c2, w_output_cross).astype(BF16)
        dq2, dk2, dv2 = cross_backward(live, q2, k2, v2, da2)
        dn2 = right_product(dq2, w_query_cross)
        dh1 = dh2 + norm_hidden_grad(h1, scale_cross, gain_cross32, dn2)
        gain_cross_terms = jnp.sum(dn2 * h1 * scale_cross, axis=0)

    with jax.named_scope("self_back_rows"):
        c1 = dh1.astype(BF16)
        da1 = product(c1, w_output_self).astype(BF16)
        da1_heads = rows_to_heads(da1)
        da1_heads = jnp.pad(da1_heads, ((0, 0), (0, broad - slim)))

    with jax.named_scope("cross_weights"):
        dkv2 = jnp.concatenate([dk2, dv2], axis=1)
        dmem = right_product(dkv2, w_key_value).astype(BF16)
        dmem = dmem.reshape(mem_count, block_width, width)
        arrived = jnp.stack(
            [dmem[0]] + [swap(dmem[mask], "mem", mask) for mask in range(1, mem_count)]
        )
        slots = memory.shape[0]
        slot_block = jnp.arange(slots, dtype=jnp.int32) * mem_count + mem_place
        slot_owner = jnp.sum((ends[None, :] <= slot_block[:, None]).astype(jnp.int32), axis=1)
        slot_row = jnp.sum(
            jnp.where(row_example[None, :] == slot_owner[:, None], places[None, :], 0), axis=1
        )
        table = jnp.stack(
            [
                lax.dynamic_index_in_dim(arrived, slot_row[s] ^ mem_place, 0, keepdims=False)
                for s in range(slots)
            ]
        )
        table = table.reshape(seq_count, (slots // seq_count) * block_width, width)
        memory_grad = functools.reduce(
            jnp.add, [piece.astype(F32) for piece in spread_seq(table)]
        ).astype(BF16)
        memory_grad = memory_grad.reshape(slots // seq_count, block_width, width)
        g_kv = left_product(turned(keys_in, 0), dkv2).astype(BF16)
        g_q2 = left_product(turned(n2, 0), dq2).astype(BF16)
        g_o2 = left_product(turned(c2, 0), a2).astype(BF16)
        g_cross = scatter_all(jnp.concatenate([g_q2, g_kv, g_o2], axis=1), back_orders[0])

    with jax.named_scope("self_back"):
        dq1, dk1, dv1 = self_backward(qkv, da1_heads, near, rows)
        dqkv = jnp.concatenate([dq1, dk1, dv1], axis=1)
        w_clean = w_self
        dn1_part = right_product(dqkv, w_clean)
        gain_self_terms = jnp.sum(dn1_part * x32 * scale_all, axis=0)
        dn1_pieces = spread_seq(dn1_part.astype(BF16).reshape(seq_count, rows, width))
        dn1 = functools.reduce(jnp.add, [piece.astype(F32) for piece in dn1_pieces])
        hidden_grad = (
            dh1 + norm_hidden_grad(x_own, norm_scale(x_own), gain_self32, dn1)
        ).astype(BF16)

    with jax.named_scope("self_weights"):
        g_qkv = left_product(turned(n1_all, 1), dqkv).astype(BF16)
        g_o1 = left_product(turned(c1, 1), a1).astype(BF16)
        g_gain = jnp.stack([gain_self_terms, gain_cross_terms, gain_feed_terms], axis=1)
        g_gain = product(
            pick[1].T,
            jnp.pad(g_gain, ((0, 0), (0, LANES - 3))).astype(BF16),
        ).astype(BF16)
        held = scatter_mem(jnp.concatenate([g_qkv, g_o1, g_gain], axis=1), back_orders[1])
        held = held.reshape(seq_count, share, held.shape[1])
        triple_held = held[:, :, : 3 * broad]
        rest_pieces = spread_seq(held[:, :, 3 * broad :])
        rest = functools.reduce(jnp.add, [piece.astype(F32) for piece in rest_pieces])
        triple_pieces = jnp.stack(spread_seq(triple_held))
        triple_back = jnp.stack(
            [
                lax.dynamic_index_in_dim(
                    triple_pieces, (seq_place - j) % seq_count, 0, keepdims=False
                )
                for j in range(seq_count)
            ],
            axis=1,
        )
        triple_back = triple_back.reshape(share, seq_count, 3, broad)[:, :, :, :slim].astype(F32)
        self_grads = [triple_back[:, :, j].reshape(share, inner) for j in range(3)]

    return (
        layer_out[None],
        hidden_grad[None],
        memory_grad,
        rest[:, inner],
        self_grads[0],
        self_grads[1],
        self_grads[2],
        rest[:, :inner],
        rest[:, inner + 1],
        g_cross[:, :inner],
        g_cross[:, inner : 2 * inner],
        g_cross[:, 2 * inner : 3 * inner],
        g_cross[:, 3 * inner :],
        rest[:, inner + 2],
        g_feed[:, :hidden_width],
        g_feed[:, hidden_width:],
        down_weight_grad,
    )


def solution(mesh):
    every = P(("mem", "seq"), None)
    gain = P(("mem", "seq"))
    in_specs = (
        (P("mem", "seq", None), P(None, "mem", None), P("mem", "seq", None), gain)
        + (every,) * 4
        + (gain,)
        + (every,) * 4
        + (gain,)
        + (every,) * 3
        + (P(),) * 3
    )
    out_specs = (
        (P("mem", "seq", None), P("mem", "seq", None), P("seq", "mem", None), gain)
        + (every,) * 4
        + (gain,)
        + (every,) * 4
        + (gain,)
        + (every,) * 3
    )
    return jax.shard_map(local, mesh=mesh, in_specs=in_specs, out_specs=out_specs, check_vma=False)
```

time: 2380 us -> 612 us (0.26)
  waiting for transfers between devices: 1940 us -> 229 us
  matrix products: 202 us -> 61.4 us
  blocking collectives: 116 us -> 0 us
  starting transfers between devices: 2.64 us -> 110 us
  Pallas kernels: 0 us -> 58.4 us
  other arithmetic: 16.2 us -> 48.5 us
    reduce_scatter x16 -> x0, waiting for transfers between devices: 1280 us -> none  [the longest x1 121 us: local(): lax.psum_scatter(up_weight_grad, ('mem', 'seq'), scatter_dimension=0, til...]
    all_gather x15 -> x0, waiting for transfers between devices: 650 us -> none  [the longest x1 57.9 us: local(): lax.all_gather(gate_weight, ('mem', 'seq'), axis=0, tiled=True)]
    ppermute x0 -> x86, waiting for transfers between devices: none -> 229 us  [the longest x41 139 us: swap(): return lax.ppermute(values, axis, [(i, i ^ mask) for i in range(size)])]
    dot_general x26 -> x8, matrix products: 142 us -> 11.6 us  [product(): return jnp.dot(left, right, preferred_element_type=F32)]
    ppermute x0 -> x86, starting transfers between devices: none -> 110 us  [the longest x45 77.6 us: shift(): lax.ppermute(values, axis, [(i, (i + step) % size) for i in range(size)])]
    unnamed x2 -> x0, blocking collectives: 82.6 us -> none
    pallas_call x0 -> x17, Pallas kernels: none -> 58.4 us  [the longest x13 20.9 us: place(): pl.pallas_call(functools.partial(place_kernel, counts, splits), out_shape...]
    pmax x1 -> x0, blocking collectives: 24 us -> none  [local(): lax.pmax(peak_table.reshape(all_rows, HEADS).astype(jnp.bfloat16), 'mem')]
  transfers between devices with their start and end apart: 31 -> 86, of which waited for: 30 -> 28; matrix products, arithmetic and copies ran while one was open for 9% -> 18% of each run, Pallas kernels for 0% -> 7%
where the time goes in v1:
time: 612 us; the launch traced here: 606 us
  waiting for transfers between devices  229 us (37%)
  starting transfers between devices  110 us (18%)
  local copies, waits for them, and re-layouts  65.8 us (11%)
  matrix products  61.4 us (10%)
  Pallas kernels  58.4 us (10%)
  other arithmetic  48.5 us (8%)
  between operations  32.3 us (5%)
    ppermute x41, waiting for transfers between devices, swap(): return lax.ppermute(values, axis, [(i, i ^ mask) for i in range(size)])  139 us
    ppermute x45, waiting for transfers between devices, shift(): lax.ppermute(values, axis, [(i, (i + step) % size) for i in range(size)])  90 us
    ppermute x45, starting transfers between devices, shift(): lax.ppermute(values, axis, [(i, (i + step) % size) for i in range(size)])  77.6 us
    ppermute x41, starting transfers between devices, swap(): return lax.ppermute(values, axis, [(i, i ^ mask) for i in range(size)])  32.9 us
    dot_general x7, matrix products, left_product(): lax.dot_general(left, right, (((0,), (0,)), ((), ())), preferred_element_...  32.6 us
    unnamed x197, local copies, waits for them, and re-layouts  23.8 us
    pallas_call x13, Pallas kernels, place(): pl.pallas_call(functools.partial(place_kernel, counts, splits), out_shape...  20.9 us
    dot_general x7, matrix products, right_product(): lax.dot_general(left, right, (((1,), (1,)), ((), ())), preferred_element_...  17.2 us
  transfers between devices with their start and end apart: 86, of which 28 were waited for; matrix products, arithmetic and copies ran while one was open for 18% of the time, Pallas kernels for 7%

profile of v1, /device:TPU:0, one launch (start us, length us, event | category | flops | bytes accessed | tf_op | source)
XLA Modules:
  0.0 605.9 jit_solution(16381492936128798705)
XLA Ops:
  96.8 26.2 %collective-permute-done.33 = bf16[24,4096]{1,0:T(8,128)(2,1)S(1)} collective-permute-done((bf16[24,4096]{1,0:T(8,128)(2,1)S(1)}, bf16[24,4096]{1,0:T(8,128)(2,1)S(1)}, u32[]{:S(2)}, u32[]{:S(2)}) %collective-permute-start.33) | collective-permute-done | bytes 196640 | tf_op jit(solution)/shard_map/gather_feed/ppermute | solution.py:56
  132.4 20.2 %collective-permute-done.7 = bf16[2,96,768]{2,1,0:T(8,128)(2,1)S(1)} collective-permute-done((bf16[2,96,768]{2,1,0:T(8,128)(2,1)S(1)}, bf16[2,96,768]{2,1,0:T(8,128)(2,1)S(1)}, u32[]{:S(2)}, u32[]{:S(2)}) %collective-permute-start.7) | collective-permute-done | bytes 294944 | tf_op jit(solution)/shard_map/gather_self/ppermute | solution.py:61
  159.7 9.1 %collective-permute-done.16 = bf16[2,96,1536]{2,1,0:T(8,128)(2,1)S(1)} collective-permute-done((bf16[2,96,1536]{2,1,0:T(8,128)(2,1)S(1)}, bf16[2,96,1536]{2,1,0:T(8,128)(2,1)S(1)}, u32[]{:S(2)}, u32[]{:S(2)}) %collective-permute-start.16) | collective-permute-done | bytes 589856 | tf_op jit(solution)/shard_map/gather_outer/ppermute | solution.py:61
  180.3 13.9 %collective-permute-done.29 = bf16[2,96,2304]{2,1,0:T(8,128)(2,1)} collective-permute-done((bf16[2,96,2304]{2,1,0:T(8,128)(2,1)}, bf16[2,96,2304]{2,1,0:T(8,128)(2,1)}, u32[]{:S(2)}, u32[]{:S(2)}) %collective-permute-start.29) | collective-permute-done | bytes 884768 | tf_op jit(solution)/shard_map/gather_cross/ppermute | solution.py:61
  195.6 7.0 %collective-permute-done.35 = bf16[2,96,4096]{2,1,0:T(8,128)(2,1)} collective-permute-done((bf16[2,96,4096]{2,1,0:T(8,128)(2,1)}, bf16[2,96,4096]{2,1,0:T(8,128)(2,1)}, u32[]{:S(2)}, u32[]{:S(2)}) %collective-permute-start.35) | collective-permute-done | bytes 1572896 | tf_op jit(solution)/shard_map/gather_feed/ppermute | solution.py:61
  208.7 6.0 self_forward.1
  217.1 10.3 %collective-permute-done.11 = bf16[256,192]{1,0:T(8,128)(2,1)S(1)} collective-permute-done((bf16[256,192]{1,0:T(8,128)(2,1)S(1)}, bf16[256,192]{1,0:T(8,128)(2,1)S(1)}, u32[]{:S(2)}, u32[]{:S(2)}) %collective-permute-start.11) | collective-permute-done | bytes 98336 | tf_op jit(solution)/shard_map/self_output/ppermute | solution.py:56
  228.1 7.7 %collective-permute-done.10 = bf16[256,192]{1,0:T(8,128)(2,1)S(1)} collective-permute-done((bf16[256,192]{1,0:T(8,128)(2,1)S(1)}, bf16[256,192]{1,0:T(8,128)(2,1)S(1)}, u32[]{:S(2)}, u32[]{:S(2)}) %collective-permute-start.10) | collective-permute-done | bytes 98336 | tf_op jit(solution)/shard_map/self_output/ppermute | solution.py:56
  236.5 6.1 %collective-permute-done.9 = bf16[256,192]{1,0:T(8,128)(2,1)S(1)} collective-permute-done((bf16[256,192]{1,0:T(8,128)(2,1)S(1)}, bf16[256,192]{1,0:T(8,128)(2,1)S(1)}, u32[]{:S(2)}, u32[]{:S(2)}) %collective-permute-start.9) | collective-permute-done | bytes 98336 | tf_op jit(solution)/shard_map/self_output/ppermute | solution.py:56
  253.6 8.5 %cross_forward.1 = bf16[256,768]{1,0:T(8,128)(2,1)S(1)} custom-call(f32[768,1]{1,0:T(8,128)S(1)} %reshape.396.live_ref, bf16[256,768]{1,0:T(8,128)(2,1)S(1)} %convolution_convert_fusion.11.q_ref, bf16[768,768]{1,0:T(8,128)(2,1)S(1)} %get-tuple-element.51.k_ref, bf16[768,768]{1,0:T(8,128)(2,1)S(1)} %get-tuple-element.50.v_ref), custom_call_target="tpu_custom_call" | custom-call | tf_op jit(solution)/shard_map/cross_attention/cross_forward/pallas_call | solution.py:328
  272.8 13.7 %cross_backward.1 = (bf16[256,768]{1,0:T(8,128)(2,1)S(1)}, bf16[768,768]{1,0:T(8,128)(2,1)S(1)}, bf16[768,768]{1,0:T(8,128)(2,1)S(1)}) custom-call(f32[768,1]{1,0:T(8,128)S(1)} %reshape.396.live_ref, bf16[256,768]{1,0:T(8,128)(2,1)S(1)} %convolution_convert_fusion.11.q_ref, bf16[768,768]{1,0:T(8,128)(2,1)S(1)} %get-tuple-element.51.k_ref, ...), custom_call_target="tpu_custom_call" | custom-call | tf_op jit(solution)/shard_map/cross_back/cross_backward/pallas_call | solution.py:341
  295.1 7.5 %convolution_convert_fusion.2 = bf16[768,1536]{1,0:T(8,128)(2,1)} fusion(bf16[768,1536]{1,0:T(8,128)(2,1)} %copy-done.41, bf16[768,768]{1,0:T(8,128)(2,1)} %copy-done.62, s32[768]{0:T(1024)} %fusion.102), kind=kOutput, calls=%fused_computation.5 | convolution fusion | flops 2720268288 | bytes 5901312 | tf_op jit(solution)/shard_map/cross_weights/dot_general | solution.py:24
  316.8 6.9 %convolution_convert_fusion = bf16[768,4096]{1,0:T(8,128)(2,1)} fusion(bf16[256,2048]{1,0:T(8,128)(2,1)} %copy-done.82, bf16[256,2048]{1,0:T(8,128)(2,1)} %copy-done.81, s32[768]{0:T(1024)} %fusion.103, f32[256,768]{1,0:T(8,128)} %copy-done.17, f32[768]{0:T(1024)S(1)} %copy-done.44, f32[256]{0:T(256)S(1)} %copy-done.64), kind=kOutput, calls=%fused_computation | convolution fusion | flops 1921318912 | bytes 9182208 | tf_op jit(solution)/shard_map/feed_back/dot_general | solution.py:24
  323.7 4.3 fusion.35
  341.3 4.1 pad_maximum_fusion
  354.9 9.4 %self_backward.1 = (bf16[1024,256]{1,0:T(8,128)(2,1)S(1)}, bf16[1024,256]{1,0:T(8,128)(2,1)S(1)}, bf16[1024,256]{1,0:T(8,128)(2,1)S(1)}) custom-call(bf16[1024,768]{1,0:T(8,128)(2,1)S(1)} %convolution_convert_fusion.4.q_ref.k_ref.v_ref, bf16[1024,768]{1,0:T(8,128)(2,1)S(1)} %convolution_convert_fusion.4.q_ref.k_ref.v_ref, ...), custom_call_target="tpu_custom_call" | custom-call | tf_op jit(solution)/shard_map/self_back/self_backward/pallas_call | solution.py:302
  368.9 7.2 %convolution_convert_fusion.8 = bf16[768,768]{0,1:T(8,128)(2,1)} fusion(bf16[1024,768]{1,0:T(8,128)(2,1)S(1)} %constant_dynamic-update-slice_fusion.14, bf16[1024,768]{1,0:T(8,128)(2,1)} %get-tuple-element.52, s32[768]{0:T(1024)S(1)} %copy-done.71), kind=kOutput, calls=%fused_computation.64 | convolution fusion | flops 2417885184 | bytes 4328448 | tf_op jit(solution)/shard_map/self_weights/dot_general | solution.py:24
  398.8 4.1 collective-permute-done.57
  402.9 15.8 %collective-permute-start.56 = (bf16[96,768]{1,0:T(8,128)(2,1)S(1)}, bf16[96,768]{1,0:T(8,128)(2,1)S(1)}, u32[]{:S(2)}, u32[]{:S(2)}) collective-permute-start(bf16[96,768]{1,0:T(8,128)(2,1)S(1)} %get-tuple-element.73), channel_id=1, source_target_pairs={{0,1},{1,2},{2,3},{3,0},{4,5},{5,6},{6,7},{7,4},{8,9},{9,10},{10,1... | collective-permute-start | bytes 442376 | tf_op jit(solution)/shard_map/cross_weights/ppermute | solution.py:56
  424.1 4.9 collective-permute-done.56
  430.3 9.0 %collective-permute-done.47 = bf16[256,768]{1,0:T(8,128)(2,1)S(1)} collective-permute-done((bf16[256,768]{1,0:T(8,128)(2,1)S(1)}, bf16[256,768]{1,0:T(8,128)(2,1)S(1)}, u32[]{:S(2)}, u32[]{:S(2)}) %collective-permute-start.47) | collective-permute-done | bytes 393248 | tf_op jit(solution)/shard_map/self_back/ppermute | solution.py:56
  445.2 13.7 %collective-permute-done.60 = bf16[192,1664]{1,0:T(8,128)(2,1)} collective-permute-done((bf16[192,1664]{1,0:T(8,128)(2,1)S(1)}, bf16[192,1664]{1,0:T(8,128)(2,1)}, u32[]{:S(2)}, u32[]{:S(2)}) %collective-permute-start.60) | collective-permute-done | bytes 639008 | tf_op jit(solution)/shard_map/self_weights/ppermute | solution.py:61
  466.4 7.1 %collective-permute-done.61 = bf16[96,1664]{0,1:T(8,128)(2,1)S(1)} collective-permute-done((bf16[96,1664]{0,1:T(8,128)(2,1)S(1)}, bf16[96,1664]{0,1:T(8,128)(2,1)S(1)}, u32[]{:S(2)}, u32[]{:S(2)}) %collective-permute-start.61) | collective-permute-done | bytes 319520 | tf_op jit(solution)/shard_map/self_weights/ppermute | solution.py:61
  474.6 4.1 collective-permute-start.67
  482.1 7.1 %collective-permute-done.81 = bf16[512,768]{1,0:T(8,128)(2,1)} collective-permute-done((bf16[512,768]{1,0:T(8,128)(2,1)S(1)}, bf16[512,768]{1,0:T(8,128)(2,1)}, u32[]{:S(2)}, u32[]{:S(2)}) %collective-permute-start.81) | collective-permute-done | bytes 786464 | tf_op jit(solution)/shard_map/feed_back/ppermute | solution.py:61
  505.4 4.0 add_convert_fusion
  509.5 13.7 %collective-permute-done.69 = bf16[192,3072]{1,0:T(8,128)(2,1)} collective-permute-done((bf16[192,3072]{1,0:T(8,128)(2,1)}, bf16[192,3072]{1,0:T(8,128)(2,1)}, u32[]{:S(2)}, u32[]{:S(2)}) %collective-permute-start.69) | collective-permute-done | bytes 1179680 | tf_op jit(solution)/shard_map/cross_weights/ppermute | solution.py:61
  533.1 36.1 %collective-permute-done.70 = bf16[96,3072]{1,0:T(8,128)(2,1)S(1)} collective-permute-done((bf16[96,3072]{1,0:T(8,128)(2,1)S(1)}, bf16[96,3072]{1,0:T(8,128)(2,1)S(1)}, u32[]{:S(2)}, u32[]{:S(2)}) %collective-permute-start.70) | collective-permute-done | bytes 589856 | tf_op jit(solution)/shard_map/cross_weights/ppermute | solution.py:61
  577.0 4.7 collective-permute-done.72
  581.8 6.6 %collective-permute-done.76 = bf16[96,4096]{1,0:T(8,128)(2,1)S(1)} collective-permute-done((bf16[96,4096]{1,0:T(8,128)(2,1)S(1)}, bf16[96,4096]{1,0:T(8,128)(2,1)S(1)}, u32[]{:S(2)}, u32[]{:S(2)}) %collective-permute-start.76) | collective-permute-done | bytes 786464 | tf_op jit(solution)/shard_map/feed_back/ppermute | solution.py:61
  593.8 3.8 collective-permute-done.79
  597.6 7.1 %collective-permute-done.78 = bf16[24,4096]{1,0:T(8,128)(2,1)S(1)} collective-permute-done((bf16[24,4096]{1,0:T(8,128)(2,1)S(1)}, bf16[24,4096]{1,0:T(8,128)(2,1)S(1)}, u32[]{:S(2)}, u32[]{:S(2)}) %collective-permute-start.78) | collective-permute-done | bytes 196640 | tf_op jit(solution)/shard_map/feed_back/ppermute | solution.py:56
  (529 shorter events, 263.6 us)
Async XLA Ops:
  2.4 56.2 %collective-permute-start.12 = (bf16[24,1536]{1,0:T(8,128)(2,1)S(1)}, bf16[24,1536]{1,0:T(8,128)(2,1)S(1)}, u32[]{:S(2)}, u32[]{:S(2)}) collective-permute-start(bf16[24,1536]{1,0:T(8,128)(2,1)S(1)} %constant_dynamic-update-slice_fusion), channel_id=1, source_target_pairs={{0,1},{1,2},{2,3},{3,0},{4,5},{5,6},{6,7},{7,4},{8,9},{9,10},{10,1... | collective-permute-start | bytes 221192 | tf_op jit(solution)/shard_map/gather_outer/ppermute | solution.py:56
  5.4 54.2 %collective-permute-start.13 = (bf16[24,1536]{1,0:T(8,128)(2,1)S(1)}, bf16[24,1536]{1,0:T(8,128)(2,1)S(1)}, u32[]{:S(2)}, u32[]{:S(2)}) collective-permute-start(bf16[24,1536]{1,0:T(8,128)(2,1)S(1)} %constant_dynamic-update-slice_fusion), channel_id=1, source_target_pairs={{0,2},{1,3},{2,0},{3,1},{4,6},{5,7},{6,4},{7,5},{8,10},{9,11},{10,... | collective-permute-start | bytes 221192 | tf_op jit(solution)/shard_map/gather_outer/ppermute | solution.py:56
  13.3 41.2 %collective-permute-start.3 = (bf16[24,768]{1,0:T(8,128)(2,1)S(1)}, bf16[24,768]{1,0:T(8,128)(2,1)S(1)}, u32[]{:S(2)}, u32[]{:S(2)}) collective-permute-start(bf16[24,768]{1,0:T(8,128)(2,1)S(1)} %get-tuple-element.120), channel_id=1, source_target_pairs={{0,1},{1,2},{2,3},{3,0},{4,5},{5,6},{6,7},{7,4},{8,9},{9,10},{10,1... | collective-permute-start | bytes 110600 | tf_op jit(solution)/shard_map/gather_self/ppermute | solution.py:56
  13.3 41.8 %collective-permute-start.4 = (bf16[24,768]{1,0:T(8,128)(2,1)S(1)}, bf16[24,768]{1,0:T(8,128)(2,1)S(1)}, u32[]{:S(2)}, u32[]{:S(2)}) collective-permute-start(bf16[24,768]{1,0:T(8,128)(2,1)S(1)} %get-tuple-element.119), channel_id=1, source_target_pairs={{0,2},{1,3},{2,0},{3,1},{4,6},{5,7},{6,4},{7,5},{8,10},{9,11},{10,... | collective-permute-start | bytes 110600 | tf_op jit(solution)/shard_map/gather_self/ppermute | solution.py:56
  15.2 41.3 %collective-permute-start.5 = (bf16[24,768]{1,0:T(8,128)(2,1)S(1)}, bf16[24,768]{1,0:T(8,128)(2,1)S(1)}, u32[]{:S(2)}, u32[]{:S(2)}) collective-permute-start(bf16[24,768]{1,0:T(8,128)(2,1)S(1)} %get-tuple-element.118), channel_id=1, source_target_pairs={{0,3},{1,0},{2,1},{3,2},{4,7},{5,4},{6,5},{7,6},{8,11},{9,8},{10,9... | collective-permute-start | bytes 110600 | tf_op jit(solution)/shard_map/gather_self/ppermute | solution.py:56
  87.0 38.8 %collective-permute-start.15 = (bf16[1,96,1536]{2,1,0:T(8,128)(2,1)S(1)}, bf16[1,96,1536]{2,1,0:T(8,128)(2,1)S(1)}, u32[]{:S(2)}, u32[]{:S(2)}) collective-permute-start(bf16[1,96,1536]{2,1,0:T(8,128)(2,1)S(1)} %bitcast.299), channel_id=1, source_target_pairs={{0,16},{4,20},{8,24},{12,28},{16,0},{20,4},{24,8},{28,12},{1,17},{... | collective-permute-start | bytes 884744 | tf_op jit(solution)/shard_map/gather_outer/ppermute | solution.py:61
  89.4 37.1 %collective-permute-start = (bf16[256,768]{1,0:T(8,128)(2,1)S(1)}, bf16[256,768]{1,0:T(8,128)(2,1)S(1)}, u32[]{:S(2)}, u32[]{:S(2)}) collective-permute-start(bf16[256,768]{1,0:T(8,128)(2,1)S(1)} %bitcast.294), channel_id=1, source_target_pairs={{0,1},{1,2},{2,3},{3,0},{4,5},{5,6},{6,7},{7,4},{8,9},{9,10},{10,1... | collective-permute-start | bytes 1179656 | tf_op jit(solution)/shard_map/gather_hidden/ppermute | solution.py:56
  91.4 36.4 %collective-permute-start.1 = (bf16[256,768]{1,0:T(8,128)(2,1)S(1)}, bf16[256,768]{1,0:T(8,128)(2,1)S(1)}, u32[]{:S(2)}, u32[]{:S(2)}) collective-permute-start(bf16[256,768]{1,0:T(8,128)(2,1)S(1)} %bitcast.295), channel_id=1, source_target_pairs={{0,2},{1,3},{2,0},{3,1},{4,6},{5,7},{6,4},{7,5},{8,10},{9,11},{10,... | collective-permute-start | bytes 1179656 | tf_op jit(solution)/shard_map/gather_hidden/ppermute | solution.py:56
  94.1 34.4 %collective-permute-start.2 = (bf16[256,768]{1,0:T(8,128)(2,1)S(1)}, bf16[256,768]{1,0:T(8,128)(2,1)S(1)}, u32[]{:S(2)}, u32[]{:S(2)}) collective-permute-start(bf16[256,768]{1,0:T(8,128)(2,1)S(1)} %bitcast.296), channel_id=1, source_target_pairs={{0,3},{1,0},{2,1},{3,2},{4,7},{5,4},{6,5},{7,6},{8,11},{9,8},{10,9... | collective-permute-start | bytes 1179656 | tf_op jit(solution)/shard_map/gather_hidden/ppermute | solution.py:56
  123.0 81.3 %collective-permute-start.22 = (bf16[96,768]{1,0:T(8,128)(2,1)}, bf16[96,768]{1,0:T(8,128)(2,1)}, u32[]{:S(2)}, u32[]{:S(2)}) collective-permute-start(bf16[96,768]{1,0:T(8,128)(2,1)} %get-tuple-element.77), channel_id=1, source_target_pairs={{0,20},{4,16},{8,28},{12,24},{16,4},{20,0},{24,12},{28,8},{1,21},{... | collective-permute-start | bytes 442376 | tf_op jit(solution)/shard_map/gather_memory/ppermute | solution.py:61
  157.8 44.8 %collective-permute-start.35 = (bf16[2,96,4096]{2,1,0:T(8,128)(2,1)}, bf16[2,96,4096]{2,1,0:T(8,128)(2,1)}, u32[]{:S(2)}, u32[]{:S(2)}) collective-permute-start(bf16[2,96,4096]{2,1,0:T(8,128)(2,1)} %pad_maximum_fusion.5), channel_id=1, source_target_pairs={{0,8},{4,12},{8,0},{12,4},{16,24},{20,28},{24,16},{28,20},{1,9},{5... | collective-permute-start | bytes 4718600 | tf_op jit(solution)/shard_map/gather_feed/ppermute | solution.py:61
  171.4 35.1 %collective-permute-start.23 = (bf16[96,768]{1,0:T(8,128)(2,1)}, bf16[96,768]{1,0:T(8,128)(2,1)S(1)}, u32[]{:S(2)}, u32[]{:S(2)}) collective-permute-start(bf16[96,768]{1,0:T(8,128)(2,1)} %get-tuple-element.82), channel_id=1, source_target_pairs={{0,24},{4,28},{8,16},{12,20},{16,8},{20,12},{24,0},{28,4},{1,25},{... | collective-permute-start | bytes 442376 | tf_op jit(solution)/shard_map/gather_memory/ppermute | solution.py:61
  178.4 36.3 %collective-permute-start.24 = (bf16[96,768]{1,0:T(8,128)(2,1)}, bf16[96,768]{1,0:T(8,128)(2,1)S(1)}, u32[]{:S(2)}, u32[]{:S(2)}) collective-permute-start(bf16[96,768]{1,0:T(8,128)(2,1)} %get-tuple-element.76), channel_id=1, source_target_pairs={{0,28},{4,24},{8,20},{12,16},{16,12},{20,8},{24,4},{28,0},{1,29},{... | collective-permute-start | bytes 442376 | tf_op jit(solution)/shard_map/gather_memory/ppermute | solution.py:61
  194.3 48.5 %collective-permute-start.17 = (bf16[4,96,1536]{2,1,0:T(8,128)(2,1)}, bf16[4,96,1536]{2,1,0:T(8,128)(2,1)S(1)}, u32[]{:S(2)}, u32[]{:S(2)}) collective-permute-start(bf16[4,96,1536]{2,1,0:T(8,128)(2,1)} %pad_maximum_fusion.9.refs_0_), channel_id=1, source_target_pairs={{0,4},{4,0},{8,12},{12,8},{16,20},{20,16},{24,28},{28,24},{1,5},{5... | collective-permute-start | bytes 3538952 | tf_op jit(solution)/shard_map/gather_outer/ppermute | solution.py:61
  202.6 44.1 %collective-permute-start.42 = (bf16[4,256,768]{2,1,0:T(8,128)(2,1)S(1)}, bf16[4,256,768]{2,1,0:T(8,128)(2,1)S(1)}, u32[]{:S(2)}, u32[]{:S(2)}) collective-permute-start(bf16[4,256,768]{2,1,0:T(8,128)(2,1)S(1)} %pad_maximum_fusion.6.refs_0_), channel_id=1, source_target_pairs={{0,4},{4,0},{8,12},{12,8},{16,20},{20,16},{24,28},{28,24},{1,5},{5... | collective-permute-start | bytes 4718600 | tf_op jit(solution)/shard_map/gather_feed/ppermute | solution.py:61
  204.3 44.5 %collective-permute-start.30 = (bf16[4,96,2304]{2,1,0:T(8,128)(2,1)S(1)}, bf16[4,96,2304]{2,1,0:T(8,128)(2,1)S(1)}, u32[]{:S(2)}, u32[]{:S(2)}) collective-permute-start(bf16[4,96,2304]{2,1,0:T(8,128)(2,1)S(1)} %pad_maximum_fusion.4.refs_0_), channel_id=1, source_target_pairs={{0,4},{4,0},{8,12},{12,8},{16,20},{20,16},{24,28},{28,24},{1,5},{5... | collective-permute-start | bytes 5308424 | tf_op jit(solution)/shard_map/gather_cross/ppermute | solution.py:61
  206.6 56.3 %collective-permute-start.36 = (bf16[4,96,4096]{2,1,0:T(8,128)(2,1)S(1)}, bf16[4,96,4096]{2,1,0:T(8,128)(2,1)S(1)}, u32[]{:S(2)}, u32[]{:S(2)}) collective-permute-start(bf16[4,96,4096]{2,1,0:T(8,128)(2,1)S(1)} %pad_maximum_fusion.1.refs_0_), channel_id=1, source_target_pairs={{0,4},{4,0},{8,12},{12,8},{16,20},{20,16},{24,28},{28,24},{1,5},{5... | collective-permute-start | bytes 9437192 | tf_op jit(solution)/shard_map/gather_feed/ppermute | solution.py:61
  339.0 40.0 %collective-permute-start.49 = (bf16[96,768]{1,0:T(8,128)(2,1)}, bf16[96,768]{1,0:T(8,128)(2,1)}, u32[]{:S(2)}, u32[]{:S(2)}) collective-permute-start(bf16[96,768]{1,0:T(8,128)(2,1)} %get-tuple-element.66), channel_id=1, source_target_pairs={{0,4},{4,0},{8,12},{12,8},{16,20},{20,16},{24,28},{28,24},{1,5},{5... | collective-permute-start | bytes 442376 | tf_op jit(solution)/shard_map/cross_weights/ppermute | solution.py:61
  351.1 34.5 %collective-permute-start.52 = (bf16[96,768]{1,0:T(8,128)(2,1)}, bf16[96,768]{1,0:T(8,128)(2,1)}, u32[]{:S(2)}, u32[]{:S(2)}) collective-permute-start(bf16[96,768]{1,0:T(8,128)(2,1)} %get-tuple-element.63), channel_id=1, source_target_pairs={{0,16},{4,20},{8,24},{12,28},{16,0},{20,4},{24,8},{28,12},{1,17},{... | collective-permute-start | bytes 442376 | tf_op jit(solution)/shard_map/cross_weights/ppermute | solution.py:61
  351.6 35.0 %collective-permute-start.53 = (bf16[96,768]{1,0:T(8,128)(2,1)}, bf16[96,768]{1,0:T(8,128)(2,1)}, u32[]{:S(2)}, u32[]{:S(2)}) collective-permute-start(bf16[96,768]{1,0:T(8,128)(2,1)} %get-tuple-element.62), channel_id=1, source_target_pairs={{0,20},{4,16},{8,28},{12,24},{16,4},{20,0},{24,12},{28,8},{1,21},{... | collective-permute-start | bytes 442376 | tf_op jit(solution)/shard_map/cross_weights/ppermute | solution.py:61
  384.4 55.4 %collective-permute-start.59 = (bf16[384,1664]{0,1:T(8,128)(2,1)S(1)}, bf16[384,1664]{0,1:T(8,128)(2,1)S(1)}, u32[]{:S(2)}, u32[]{:S(2)}) collective-permute-start(bf16[384,1664]{0,1:T(8,128)(2,1)S(1)} %slice.293), channel_id=1, source_target_pairs={{0,4},{4,0},{8,12},{12,8},{16,20},{20,16},{24,28},{28,24},{1,5},{5... | collective-permute-start | bytes 3833864 | tf_op jit(solution)/shard_map/self_weights/ppermute | solution.py:61
  395.3 34.5 %collective-permute-start.48 = (bf16[256,768]{1,0:T(8,128)(2,1)S(1)}, bf16[256,768]{1,0:T(8,128)(2,1)S(1)}, u32[]{:S(2)}, u32[]{:S(2)}) collective-permute-start(bf16[256,768]{1,0:T(8,128)(2,1)S(1)} %get-tuple-element.54), channel_id=1, source_target_pairs={{0,3},{1,0},{2,1},{3,2},{4,7},{5,4},{6,5},{7,6},{8,11},{9,8},{10,9... | collective-permute-start | bytes 1179656 | tf_op jit(solution)/shard_map/self_back/ppermute | solution.py:56
  397.7 41.6 %collective-permute-start.47 = (bf16[256,768]{1,0:T(8,128)(2,1)S(1)}, bf16[256,768]{1,0:T(8,128)(2,1)S(1)}, u32[]{:S(2)}, u32[]{:S(2)}) collective-permute-start(bf16[256,768]{1,0:T(8,128)(2,1)S(1)} %get-tuple-element.55), channel_id=1, source_target_pairs={{0,2},{1,3},{2,0},{3,1},{4,6},{5,7},{6,4},{7,5},{8,10},{9,11},{10,... | collective-permute-start | bytes 1179656 | tf_op jit(solution)/shard_map/self_back/ppermute | solution.py:56
  398.8 40.6 %collective-permute-start.46 = (bf16[256,768]{1,0:T(8,128)(2,1)S(1)}, bf16[256,768]{1,0:T(8,128)(2,1)S(1)}, u32[]{:S(2)}, u32[]{:S(2)}) collective-permute-start(bf16[256,768]{1,0:T(8,128)(2,1)S(1)} %get-tuple-element.53), channel_id=1, source_target_pairs={{0,1},{1,2},{2,3},{3,0},{4,5},{5,6},{6,7},{7,4},{8,9},{9,10},{10,1... | collective-permute-start | bytes 1179656 | tf_op jit(solution)/shard_map/self_back/ppermute | solution.py:56
  429.0 49.6 %collective-permute-start.68 = (bf16[384,3072]{1,0:T(8,128)(2,1)}, bf16[384,3072]{1,0:T(8,128)(2,1)}, u32[]{:S(2)}, u32[]{:S(2)}) collective-permute-start(bf16[384,3072]{1,0:T(8,128)(2,1)} %slice.304), channel_id=1, source_target_pairs={{0,4},{4,0},{8,12},{12,8},{16,20},{20,16},{24,28},{28,24},{1,5},{5... | collective-permute-start | bytes 7077896 | tf_op jit(solution)/shard_map/cross_weights/ppermute | solution.py:61
  429.8 75.0 %collective-permute-start.74 = (bf16[384,4096]{1,0:T(8,128)(2,1)}, bf16[384,4096]{1,0:T(8,128)(2,1)}, u32[]{:S(2)}, u32[]{:S(2)}) collective-permute-start(bf16[384,4096]{1,0:T(8,128)(2,1)} %slice.315), channel_id=1, source_target_pairs={{0,4},{4,0},{8,12},{12,8},{16,20},{20,16},{24,28},{28,24},{1,5},{5... | collective-permute-start | bytes 9437192 | tf_op jit(solution)/shard_map/feed_back/ppermute | solution.py:61
  474.6 50.9 %collective-permute-start.64 = (bf16[24,896]{1,0:T(8,128)(2,1)}, bf16[24,896]{1,0:T(8,128)(2,1)}, u32[]{:S(2)}, u32[]{:S(2)}) collective-permute-start(bf16[24,896]{1,0:T(8,128)(2,1)} %get-tuple-element.108), channel_id=1, source_target_pairs={{0,3},{1,0},{2,1},{3,2},{4,7},{5,4},{6,5},{7,6},{8,11},{9,8},{10,9... | collective-permute-start | bytes 129032 | tf_op jit(solution)/shard_map/self_weights/ppermute | solution.py:56
  523.2 48.7 %collective-permute-start.75 = (bf16[192,4096]{1,0:T(8,128)(2,1)S(1)}, bf16[192,4096]{1,0:T(8,128)(2,1)S(1)}, u32[]{:S(2)}, u32[]{:S(2)}) collective-permute-start(bf16[192,4096]{1,0:T(8,128)(2,1)S(1)} %slice.317), channel_id=1, source_target_pairs={{0,16},{4,20},{8,24},{12,28},{16,0},{20,4},{24,8},{28,12},{1,17},{... | collective-permute-start | bytes 4718600 | tf_op jit(solution)/shard_map/feed_back/ppermute | solution.py:61
  525.4 43.7 %collective-permute-start.70 = (bf16[96,3072]{1,0:T(8,128)(2,1)S(1)}, bf16[96,3072]{1,0:T(8,128)(2,1)S(1)}, u32[]{:S(2)}, u32[]{:S(2)}) collective-permute-start(bf16[96,3072]{1,0:T(8,128)(2,1)S(1)} %slice.308), channel_id=1, source_target_pairs={{0,16},{4,20},{8,24},{12,28},{16,0},{20,4},{24,8},{28,12},{1,17},{... | collective-permute-start | bytes 1769480 | tf_op jit(solution)/shard_map/cross_weights/ppermute | solution.py:61
  529.4 43.1 %collective-permute-start.85 = (bf16[64,768]{1,0:T(8,128)(2,1)S(1)}, bf16[64,768]{1,0:T(8,128)(2,1)S(1)}, u32[]{:S(2)}, u32[]{:S(2)}) collective-permute-start(bf16[64,768]{1,0:T(8,128)(2,1)S(1)} %get-tuple-element.92), channel_id=1, source_target_pairs={{0,3},{1,0},{2,1},{3,2},{4,7},{5,4},{6,5},{7,6},{8,11},{9,8},{10,9... | collective-permute-start | bytes 294920 | tf_op jit(solution)/shard_map/feed_back/ppermute | solution.py:56
  531.7 42.0 %collective-permute-start.84 = (bf16[64,768]{1,0:T(8,128)(2,1)S(1)}, bf16[64,768]{1,0:T(8,128)(2,1)S(1)}, u32[]{:S(2)}, u32[]{:S(2)}) collective-permute-start(bf16[64,768]{1,0:T(8,128)(2,1)S(1)} %get-tuple-element.93), channel_id=1, source_target_pairs={{0,2},{1,3},{2,0},{3,1},{4,6},{5,7},{6,4},{7,5},{8,10},{9,11},{10,... | collective-permute-start | bytes 294920 | tf_op jit(solution)/shard_map/feed_back/ppermute | solution.py:56
  531.7 43.2 %collective-permute-start.83 = (bf16[64,768]{1,0:T(8,128)(2,1)S(1)}, bf16[64,768]{1,0:T(8,128)(2,1)S(1)}, u32[]{:S(2)}, u32[]{:S(2)}) collective-permute-start(bf16[64,768]{1,0:T(8,128)(2,1)S(1)} %get-tuple-element.91), channel_id=1, source_target_pairs={{0,1},{1,2},{2,3},{3,0},{4,5},{5,6},{6,7},{7,4},{8,9},{9,10},{10,1... | collective-permute-start | bytes 294920 | tf_op jit(solution)/shard_map/feed_back/ppermute | solution.py:56
  (141 other events, 2270.9 us)
